TPU v7x, 256 devices: a whole 4x4x8 slice. The times are simulated.
256 devices in a mesh: gx: 32 (over x, z), gy: 8 (over y, core).
Axes of the slice: x: 4, y: 4, z: 8, core: 2. Of those that a mesh axis runs over, the one named last changes fastest.
Arguments:
- order_params: float32 [24, 12, 256, 1024], P(None, None, 'gx', 'gy'), may hold values from 0 to 1, as said below
- grain_ids: int32 [32, 8, 24], P('gx', 'gy'), may hold values from -1 to 9215, as said below
- channel_maps: int32 [32, 8, 4, 24], P('gx', 'gy'), may hold values from -1 to 23, as said below
- zplanes: int32 [2, 256, 1024], P(None, 'gx', 'gy'), may hold values from 0 to 9215, as said below
Outputs:
- evolved: float32 [24, 12, 256, 1024], P(None, None, 'gx', 'gy')
Inputs may be any that keep to these rules, and one draw needn't show every extreme that they name: `order_params`: zero in every slot whose grain id is -1. `grain_ids`: grain ids are distinct within a block; -1 marks an empty slot. `channel_maps`: A non-negative entry for face f of a block names the adjacent block's slot with the same grain; the entries for face f of a block and for the opposite face of the adjacent block are inverse one-to-one matchings. At most 6 slots of a block have an entry for any one face, and in every draw some face of some block has exactly 6. A slot has an entry for at most one face. `zplanes`: each cell names one of the non-negative grain ids of its block.
All inputs are finite; a program needn't handle non-finite values.
Results may differ from a plain program's by a relative error of at most 0.00018.
Values sent between devices are 32-bit elements; how exact they have to be, the bound alone decides.
A program may use at most 64 MiB of HBM per device.

v0:
```python
import jax
import jax.numpy as jnp
from jax import lax
from jax.sharding import PartitionSpec as P

STEPS = 3


time_step = 0.05
mobility = 1.0
alpha_coef = 1.0
beta_coef = 1.0
gamma_coef = 1.5
kappa_coef = 2.0


def shifted(block, axis, distance):
    devices = range(lax.axis_size(axis))
    route = [((i - distance) % len(devices), i) for i in devices]
    return lax.ppermute(block, axis, route)


def reorder(rim, partner):
    count = rim.shape[0]
    select = (partner[:, None] == jnp.arange(count, dtype=jnp.int32)[None, :]).astype(jnp.float32)
    return jnp.einsum("st,tzc->szc", select, rim, precision=lax.Precision.HIGHEST)


def advance(field, lower_x, upper_x, lower_y, upper_y, frozen):
    depth, rows, cols = (field.shape[1], field.shape[2], field.shape[3])
    row_index = lax.broadcasted_iota(jnp.int32, (1, 1, rows, 1), 2)
    col_index = lax.broadcasted_iota(jnp.int32, (1, 1, 1, cols), 3)
    layer_index = lax.broadcasted_iota(jnp.int32, (1, depth, 1, 1), 1)
    above_x = jnp.where(row_index == rows - 1, upper_x[:, :, None, :], jnp.roll(field, -1, axis=2))
    below_x = jnp.where(row_index == 0, lower_x[:, :, None, :], jnp.roll(field, 1, axis=2))
    above_y = jnp.where(col_index == cols - 1, upper_y[..., None], jnp.roll(field, -1, axis=3))
    below_y = jnp.where(col_index == 0, lower_y[..., None], jnp.roll(field, 1, axis=3))
    above_z = jnp.where(layer_index == depth - 1, frozen[1][:, None], jnp.roll(field, -1, axis=1))
    below_z = jnp.where(layer_index == 0, frozen[0][:, None], jnp.roll(field, 1, axis=1))
    laplace = above_x + below_x + above_y + below_y + above_z + below_z - 6.0 * field
    total = jnp.sum(field * field, axis=0, keepdims=True)
    rate = (
        -alpha_coef * field
        + beta_coef * field**3
        + 2.0 * gamma_coef * field * (total - field * field)
        - kappa_coef * laplace
    )
    return field - time_step * mobility * rate


def on_device(order_params, grain_ids, channel_maps, zplanes):
    slot_grains = grain_ids[0, 0]
    face_maps = channel_maps[0, 0]
    matches = zplanes[:, None, :, :] == slot_grains[None, :, None, None]
    frozen = (matches & (slot_grains[None, :, None, None] >= 0)).astype(jnp.float32)
    field = order_params
    for repeat_index in range(STEPS):
        lower_x = reorder(shifted(field[:, :, -1, :], "gx", 1), face_maps[0])
        upper_x = reorder(shifted(field[:, :, 0, :], "gx", -1), face_maps[1])
        lower_y = reorder(shifted(field[:, :, :, -1], "gy", 1), face_maps[2])
        upper_y = reorder(shifted(field[:, :, :, 0], "gy", -1), face_maps[3])
        field = advance(field, lower_x, upper_x, lower_y, upper_y, frozen)
    return field


def solution(mesh):
    in_specs = (
        P(None, None, "gx", "gy"),
        P("gx", "gy", None),
        P("gx", "gy", None, None),
        P(None, "gx", "gy"),
    )
    out_specs = P(None, None, "gx", "gy")
    return jax.shard_map(
        on_device, mesh=mesh, in_specs=in_specs, out_specs=out_specs, check_vma=False
    )
```

profile of v0, /device:TPU:1, one launch (start us, length us, event | category | flops | bytes accessed | tf_op | source)
XLA Modules:
  0.0 92.3 jit_solution(1902418021384222140)
XLA Ops:
  0.0 2.1 %copy.45 = f32[24,12,8,128]{3,0,1,2:T(8,128)S(1)} copy(f32[24,12,8,128]{3,2,1,0:T(8,128)} %param.4) | data formatting | bytes 2359296 | tf_op args[0]
  2.1 0.9 slice_bitcast_fusion.11
  2.9 8.6 %collective-permute-start = (f32[24,12,128]{2,0,1:T(8,128)}, f32[24,12,128]{2,0,1:T(8,128)}, u32[]{:S(2)}, u32[]{:S(2)}) collective-permute-start(f32[24,12,128]{2,0,1:T(8,128)} %get-tuple-element.33), channel_id=1, source_target_pairs={{8,0},{16,8},{24,16},{32,24},{40,32},{48,40},{56,48},{64,56},{72,6... | collective-permute-start | bytes 442376 | tf_op jit(solution)/shard_map/ppermute | solution.py:20
  11.5 1.4 %fusion.98 = (f32[24,12,8,1]{3,2,1,0:T(8,128)}, f32[24,12,8,1]{3,2,1,0:T(8,128)S(1)}) fusion(f32[24,12,8,128]{3,2,1,0:T(8,128)S(1)} %copy-done), kind=kLoop, calls=%fused_computation.131 | loop fusion | bytes 36864 | tf_op jit(solution)/shard_map/slice | solution.py:60
  13.0 1.5 %copy.59 = f32[24,12,8,1]{0,1,2,3:T(8,128)} copy(f32[24,12,8,1]{3,2,1,0:T(8,128)S(1)} %get-tuple-element.42) | data formatting | bytes 18432
  14.5 1.0 %collective-permute-start.2 = (f32[24,12,8]{0,1,2:T(8,128)}, f32[24,12,8]{0,1,2:T(8,128)}, u32[]{:S(2)}, u32[]{:S(2)}) collective-permute-start(f32[24,12,8]{0,1,2:T(8,128)} %bitcast.68), channel_id=1, source_target_pairs={{1,0},{2,1},{3,2},{4,3},{5,4},{6,5},{7,6},{0,7},{9,8},{10,9},{11,1... | collective-permute-start | bytes 27656 | tf_op jit(solution)/shard_map/ppermute | solution.py:20
  15.5 2.7 %copy.60 = f32[24,12,8,1]{0,1,2,3:T(8,128)} copy(f32[24,12,8,1]{3,2,1,0:T(8,128)} %get-tuple-element.41) | data formatting | bytes 18432
  18.2 1.2 %collective-permute-start.3 = (f32[24,12,8]{0,1,2:T(8,128)}, f32[24,12,8]{0,1,2:T(8,128)S(1)}, u32[]{:S(2)}, u32[]{:S(2)}) collective-permute-start(f32[24,12,8]{0,1,2:T(8,128)} %bitcast.69), channel_id=1, source_target_pairs={{7,0},{0,1},{1,2},{2,3},{3,4},{4,5},{5,6},{6,7},{15,8},{8,9},{9,10... | collective-permute-start | bytes 27656 | tf_op jit(solution)/shard_map/ppermute | solution.py:20
  19.8 0.4 fusion.99
  20.7 0.4 copy-done.1
  21.1 0.7 copy.39
  21.8 0.7 copy.36
  22.5 1.1 %fusion.64 = f32[24,12,8]{0,1,2:T(8,128)S(1)} fusion(f32[24,12,8]{0,1,2:T(8,128)} %collective-permute-done.2, s32[24]{0:T(128)S(1)} %get-tuple-element.52), kind=kOutput, calls=%fused_computation.84 | convolution fusion | flops 664128 | bytes 18528 | tf_op jit(solution)/shard_map/st,tzc->szc/dot_general | solution.py:26
  23.9 1.2 %fusion.50 = f32[24,12,128]{2,0,1:T(8,128)S(1)} fusion(f32[24,12,128]{2,0,1:T(8,128)} %collective-permute-done, s32[24]{0:T(128)S(1)} %get-tuple-element.49), kind=kOutput, calls=%fused_computation.76 | convolution fusion | flops 10617408 | bytes 295008 | tf_op jit(solution)/shard_map/st,tzc->szc/dot_general | solution.py:26
  25.1 1.2 %fusion.57 = f32[24,12,128]{2,0,1:T(8,128)S(1)} fusion(f32[24,12,128]{2,0,1:T(8,128)} %collective-permute-done.1, s32[24]{0:T(128)S(1)} %get-tuple-element.50), kind=kOutput, calls=%fused_computation.80 | convolution fusion | flops 10617408 | bytes 295008 | tf_op jit(solution)/shard_map/st,tzc->szc/dot_general | solution.py:26
  26.3 4.8 %fusion.20 = f32[24,12,8,128]{3,0,1,2:T(8,128)S(1)} fusion(f32[24,12,1,128]{3,0,1,2:T(8,128)S(1)} %copy-done.4, f32[24,12,7,128]{3,0,1,2:T(8,128)S(1)} %get-tuple-element.46, f32[24,12,7,128]{3,0,1,2:T(8,128)S(1)} %get-tuple-element.45, f32[24,12,1,128]{3,0,1,2:T(8,128)S(1)} %copy-done.3, f32[24,12,8,1]{3,0,1,2:T(8,128)S(1)} %copy.36, ...), kind=kOutput, calls=%fused_computation.20 | output fusion | flops 9154583 | bytes 9947432 | tf_op jit(solution)/shard_map/sub | solution.py:45
  31.2 0.8 slice_bitcast_fusion.9
  32.0 1.6 %fusion.95 = (f32[24,12,7,128]{3,0,1,2:T(8,128)}, f32[24,12,7,128]{3,0,1,2:T(8,128)}) fusion(f32[24,12,8,128]{3,0,1,2:T(8,128)S(1)} %fusion.20), kind=kLoop, calls=%fused_computation.128 | loop fusion | bytes 4128768 | tf_op jit(solution)/shard_map/jit(_roll_static)/slice | solution.py:35
  33.6 1.5 %fusion.92 = (f32[24,11,8,128]{3,0,1,2:T(8,128)}, f32[24,11,8,128]{3,0,1,2:T(8,128)}) fusion(f32[24,12,8,128]{3,0,1,2:T(8,128)S(1)} %fusion.20), kind=kLoop, calls=%fused_computation.125 | loop fusion | bytes 4325376 | tf_op jit(solution)/shard_map/jit(_roll_static)/slice | solution.py:39
  35.1 1.8 %fusion.94 = (f32[24,12,8,127]{3,0,1,2:T(8,128)}, f32[24,12,8,127]{3,0,1,2:T(8,128)}) fusion(f32[24,12,8,128]{3,0,1,2:T(8,128)S(1)} %fusion.20), kind=kLoop, calls=%fused_computation.127 | loop fusion | bytes 4681728 | tf_op jit(solution)/shard_map/jit(_roll_static)/slice | solution.py:37
  37.3 1.4 %copy.55 = f32[24,12,8,1]{0,1,2,3:T(8,128)} copy(f32[24,12,8,1]{3,0,1,2:T(8,128)S(1)} %get-tuple-element.28) | data formatting | bytes 18432 | tf_op jit(solution)/shard_map/squeeze | solution.py:61
  38.7 1.9 %collective-permute-start.6 = (f32[24,12,8]{0,1,2:T(8,128)}, f32[24,12,8]{0,1,2:T(8,128)}, u32[]{:S(2)}, u32[]{:S(2)}) collective-permute-start(f32[24,12,8]{0,1,2:T(8,128)} %bitcast.70), channel_id=1, source_target_pairs={{1,0},{2,1},{3,2},{4,3},{5,4},{6,5},{7,6},{0,7},{9,8},{10,9},{11,1... | collective-permute-start | bytes 27656 | tf_op jit(solution)/shard_map/ppermute | solution.py:20
  40.6 0.7 fusion.91
  41.3 4.8 %collective-permute-start.4 = (f32[24,12,128]{2,0,1:T(8,128)}, f32[24,12,128]{2,0,1:T(8,128)}, u32[]{:S(2)}, u32[]{:S(2)}) collective-permute-start(f32[24,12,128]{2,0,1:T(8,128)} %get-tuple-element.19), channel_id=1, source_target_pairs={{8,0},{16,8},{24,16},{32,24},{40,32},{48,40},{56,48},{64,56},{72,6... | collective-permute-start | bytes 442376 | tf_op jit(solution)/shard_map/ppermute | solution.py:20
  46.1 1.4 %copy.56 = f32[24,12,8,1]{0,1,2,3:T(8,128)} copy(f32[24,12,8,1]{3,0,1,2:T(8,128)S(1)} %get-tuple-element.27) | data formatting | bytes 18432 | tf_op jit(solution)/shard_map/squeeze | solution.py:60
  47.5 0.4 collective-permute-start.7
  48.0 1.1 %fusion.62 = f32[24,12,8]{0,1,2:T(8,128)S(1)} fusion(f32[24,12,8]{0,1,2:T(8,128)} %collective-permute-done.6, s32[24]{0:T(128)S(1)} %get-tuple-element.52), kind=kOutput, calls=%fused_computation.83 | convolution fusion | flops 664128 | bytes 18528 | tf_op jit(solution)/shard_map/st,tzc->szc/dot_general | solution.py:26
  49.1 1.8 %collective-permute-done.7 = f32[24,12,8]{0,1,2:T(8,128)S(1)} collective-permute-done((f32[24,12,8]{0,1,2:T(8,128)}, f32[24,12,8]{0,1,2:T(8,128)S(1)}, u32[]{:S(2)}, u32[]{:S(2)}) %collective-permute-start.7) | collective-permute-done | bytes 9248 | tf_op jit(solution)/shard_map/ppermute | solution.py:20
  51.1 1.2 %fusion.48 = f32[24,12,128]{2,0,1:T(8,128)S(1)} fusion(f32[24,12,128]{2,0,1:T(8,128)} %collective-permute-done.4, s32[24]{0:T(128)S(1)} %get-tuple-element.49), kind=kOutput, calls=%fused_computation.75 | convolution fusion | flops 10617408 | bytes 295008 | tf_op jit(solution)/shard_map/st,tzc->szc/dot_general | solution.py:26
  52.3 1.4 %collective-permute-done.5 = f32[24,12,128]{2,0,1:T(8,128)} collective-permute-done((f32[24,12,128]{2,0,1:T(8,128)}, f32[24,12,128]{2,0,1:T(8,128)}, u32[]{:S(2)}, u32[]{:S(2)}) %collective-permute-start.5) | collective-permute-done | bytes 147488 | tf_op jit(solution)/shard_map/ppermute | solution.py:20
  53.7 1.2 %fusion.55 = f32[24,12,128]{2,0,1:T(8,128)S(1)} fusion(f32[24,12,128]{2,0,1:T(8,128)} %collective-permute-done.5, s32[24]{0:T(128)S(1)} %get-tuple-element.50), kind=kOutput, calls=%fused_computation.79 | convolution fusion | flops 10617408 | bytes 295008 | tf_op jit(solution)/shard_map/st,tzc->szc/dot_general | solution.py:26
  54.9 5.0 %fusion.15 = f32[24,12,8,128]{3,0,1,2:T(8,128)S(1)} fusion(f32[24,12,8,128]{3,0,1,2:T(8,128)S(1)} %fusion.20, f32[24,12,1,128]{3,0,1,2:T(8,128)} %get-tuple-element.22, f32[24,12,7,128]{3,0,1,2:T(8,128)} %get-tuple-element.32, f32[24,12,7,128]{3,0,1,2:T(8,128)} %get-tuple-element.31, f32[24,12,1,128]{3,0,1,2:T(8,128)} %get-tuple-element.21, ...), kind=kOutput, calls=%fused_computation.15 | output fusion | flops 9154583 | bytes 9947432 | tf_op jit(solution)/shard_map/sub | solution.py:45
  59.9 0.9 slice_bitcast_fusion.7
  60.8 1.5 %fusion.90 = (f32[24,12,7,128]{3,0,1,2:T(8,128)}, f32[24,12,7,128]{3,0,1,2:T(8,128)}) fusion(f32[24,12,8,128]{3,0,1,2:T(8,128)S(1)} %fusion.15), kind=kLoop, calls=%fused_computation.123 | loop fusion | bytes 4128768 | tf_op jit(solution)/shard_map/jit(_roll_static)/slice | solution.py:35
  62.4 1.5 %fusion.87 = (f32[24,11,8,128]{3,0,1,2:T(8,128)}, f32[24,11,8,128]{3,0,1,2:T(8,128)}) fusion(f32[24,12,8,128]{3,0,1,2:T(8,128)S(1)} %fusion.15), kind=kLoop, calls=%fused_computation.120 | loop fusion | bytes 4325376 | tf_op jit(solution)/shard_map/jit(_roll_static)/slice | solution.py:39
  63.8 1.8 %fusion.89 = (f32[24,12,8,127]{3,0,1,2:T(8,128)}, f32[24,12,8,127]{3,0,1,2:T(8,128)}) fusion(f32[24,12,8,128]{3,0,1,2:T(8,128)S(1)} %fusion.15), kind=kLoop, calls=%fused_computation.122 | loop fusion | bytes 4681728 | tf_op jit(solution)/shard_map/jit(_roll_static)/slice | solution.py:37
  66.0 1.4 %copy.57 = f32[24,12,8,1]{0,1,2,3:T(8,128)} copy(f32[24,12,8,1]{3,0,1,2:T(8,128)S(1)} %get-tuple-element.14) | data formatting | bytes 18432 | tf_op jit(solution)/shard_map/squeeze | solution.py:61
  67.4 3.5 %collective-permute-start.10 = (f32[24,12,8]{0,1,2:T(8,128)}, f32[24,12,8]{0,1,2:T(8,128)}, u32[]{:S(2)}, u32[]{:S(2)}) collective-permute-start(f32[24,12,8]{0,1,2:T(8,128)} %bitcast.71), channel_id=1, source_target_pairs={{1,0},{2,1},{3,2},{4,3},{5,4},{6,5},{7,6},{0,7},{9,8},{10,9},{11,1... | collective-permute-start | bytes 27656 | tf_op jit(solution)/shard_map/ppermute | solution.py:20
  71.0 0.7 fusion.86
  71.6 4.3 %collective-permute-start.8 = (f32[24,12,128]{2,0,1:T(8,128)}, f32[24,12,128]{2,0,1:T(8,128)}, u32[]{:S(2)}, u32[]{:S(2)}) collective-permute-start(f32[24,12,128]{2,0,1:T(8,128)} %get-tuple-element.5), channel_id=1, source_target_pairs={{8,0},{16,8},{24,16},{32,24},{40,32},{48,40},{56,48},{64,56},{72,6... | collective-permute-start | bytes 442376 | tf_op jit(solution)/shard_map/ppermute | solution.py:20
  75.9 1.4 %copy.58 = f32[24,12,8,1]{0,1,2,3:T(8,128)} copy(f32[24,12,8,1]{3,0,1,2:T(8,128)S(1)} %get-tuple-element.13) | data formatting | bytes 18432 | tf_op jit(solution)/shard_map/squeeze | solution.py:60
  77.4 1.1 %fusion.60 = f32[24,12,8]{0,1,2:T(8,128)S(1)} fusion(f32[24,12,8]{0,1,2:T(8,128)} %collective-permute-done.10, s32[24]{0:T(128)S(1)} %get-tuple-element.52), kind=kOutput, calls=%fused_computation.82 | convolution fusion | flops 664128 | bytes 18528 | tf_op jit(solution)/shard_map/st,tzc->szc/dot_general | solution.py:26
  78.4 0.6 collective-permute-done.11
  79.5 1.2 %fusion.46 = f32[24,12,128]{2,0,1:T(8,128)S(1)} fusion(f32[24,12,128]{2,0,1:T(8,128)} %collective-permute-done.8, s32[24]{0:T(128)S(1)} %get-tuple-element.49), kind=kOutput, calls=%fused_computation.74 | convolution fusion | flops 10617408 | bytes 295008 | tf_op jit(solution)/shard_map/st,tzc->szc/dot_general | solution.py:26
  80.7 4.0 %collective-permute-done.9 = f32[24,12,128]{2,0,1:T(8,128)} collective-permute-done((f32[24,12,128]{2,0,1:T(8,128)}, f32[24,12,128]{2,0,1:T(8,128)}, u32[]{:S(2)}, u32[]{:S(2)}) %collective-permute-start.9) | collective-permute-done | bytes 147488 | tf_op jit(solution)/shard_map/ppermute | solution.py:20
  84.7 1.2 %fusion.53 = f32[24,12,128]{2,0,1:T(8,128)S(1)} fusion(f32[24,12,128]{2,0,1:T(8,128)} %collective-permute-done.9, s32[24]{0:T(128)S(1)} %get-tuple-element.50), kind=kOutput, calls=%fused_computation.78 | convolution fusion | flops 10617408 | bytes 295008 | tf_op jit(solution)/shard_map/st,tzc->szc/dot_general | solution.py:26
  85.9 4.7 %fusion.10 = f32[24,12,8,128]{3,0,1,2:T(8,128)S(1)} fusion(f32[24,12,8,128]{3,0,1,2:T(8,128)S(1)} %fusion.15, f32[24,12,1,128]{3,0,1,2:T(8,128)} %get-tuple-element.8, f32[24,12,7,128]{3,0,1,2:T(8,128)} %get-tuple-element.18, f32[24,12,7,128]{3,0,1,2:T(8,128)} %get-tuple-element.17, f32[24,12,1,128]{3,0,1,2:T(8,128)} %get-tuple-element.7, ...), kind=kOutput, calls=%fused_computation.10 | output fusion | flops 9154583 | bytes 9947432 | tf_op jit(solution)/shard_map/sub | solution.py:45
  90.6 1.7 %copy.54 = f32[24,12,8,128]{3,2,1,0:T(8,128)} copy(f32[24,12,8,128]{3,0,1,2:T(8,128)S(1)} %fusion.10) | data formatting | bytes 2359296 | tf_op jit(solution)/shard_map/sub | solution.py:48
  (58 shorter events, 2.6 us)
Async XLA Ops:
  0.0 11.5 %copy-start = (f32[24,12,8,128]{3,2,1,0:T(8,128)S(1)}, f32[24,12,8,128]{3,2,1,0:T(8,128)}, u32[]{:S(2)}) copy-start(f32[24,12,8,128]{3,2,1,0:T(8,128)} %param.4) | copy-start | bytes 3538948
  2.9 20.9 %collective-permute-start = (f32[24,12,128]{2,0,1:T(8,128)}, f32[24,12,128]{2,0,1:T(8,128)}, u32[]{:S(2)}, u32[]{:S(2)}) collective-permute-start(f32[24,12,128]{2,0,1:T(8,128)} %get-tuple-element.33), channel_id=1, source_target_pairs={{8,0},{16,8},{24,16},{32,24},{40,32},{48,40},{56,48},{64,56},{72,6... | collective-permute-start | bytes 442376 | tf_op jit(solution)/shard_map/ppermute | solution.py:20
  11.5 13.5 %collective-permute-start.1 = (f32[24,12,128]{2,0,1:T(8,128)}, f32[24,12,128]{2,0,1:T(8,128)}, u32[]{:S(2)}, u32[]{:S(2)}) collective-permute-start(f32[24,12,128]{2,0,1:T(8,128)} %get-tuple-element.36), channel_id=1, source_target_pairs={{248,0},{0,8},{8,16},{16,24},{24,32},{32,40},{40,48},{48,56},{56,6... | collective-permute-start | bytes 442376 | tf_op jit(solution)/shard_map/ppermute | solution.py:20
  14.5 8.0 %collective-permute-start.2 = (f32[24,12,8]{0,1,2:T(8,128)}, f32[24,12,8]{0,1,2:T(8,128)}, u32[]{:S(2)}, u32[]{:S(2)}) collective-permute-start(f32[24,12,8]{0,1,2:T(8,128)} %bitcast.68), channel_id=1, source_target_pairs={{1,0},{2,1},{3,2},{4,3},{5,4},{6,5},{7,6},{0,7},{9,8},{10,9},{11,1... | collective-permute-start | bytes 27656 | tf_op jit(solution)/shard_map/ppermute | solution.py:20
  18.2 5.4 %collective-permute-start.3 = (f32[24,12,8]{0,1,2:T(8,128)}, f32[24,12,8]{0,1,2:T(8,128)S(1)}, u32[]{:S(2)}, u32[]{:S(2)}) collective-permute-start(f32[24,12,8]{0,1,2:T(8,128)} %bitcast.69), channel_id=1, source_target_pairs={{7,0},{0,1},{1,2},{2,3},{3,4},{4,5},{5,6},{6,7},{15,8},{8,9},{9,10... | collective-permute-start | bytes 27656 | tf_op jit(solution)/shard_map/ppermute | solution.py:20
  19.4 6.8 %copy-start.10 = (pred[8]{0:T(512)(128)(4,1)}, pred[8]{0:T(512)(128)(4,1)S(1)}, u32[]{:S(2)}) copy-start(pred[8]{0:T(512)(128)(4,1)S(1)} %get-tuple-element.57) | copy-start | bytes 28
  19.4 6.9 %copy-start.11 = (pred[8]{0:T(512)(128)(4,1)}, pred[8]{0:T(512)(128)(4,1)S(1)}, u32[]{:S(2)}) copy-start(pred[8]{0:T(512)(128)(4,1)S(1)} %get-tuple-element.58) | copy-start | bytes 28
  19.4 6.9 %copy-start.12 = (pred[128]{0:T(512)(128)(4,1)}, pred[128]{0:T(512)(128)(4,1)S(1)}, u32[]{:S(2)}) copy-start(pred[128]{0:T(512)(128)(4,1)S(1)} %get-tuple-element.55) | copy-start | bytes 388
  19.4 6.9 %copy-start.13 = (pred[128]{0:T(512)(128)(4,1)}, pred[128]{0:T(512)(128)(4,1)S(1)}, u32[]{:S(2)}) copy-start(pred[128]{0:T(512)(128)(4,1)S(1)} %get-tuple-element.56) | copy-start | bytes 388
  19.8 0.7 copy-start.9
  19.8 0.7 copy-start.8
  19.8 0.7 copy-start.7
  19.8 1.3 %copy-start.1 = (f32[24,12,8,1]{3,2,1,0:T(8,128)S(1)}, f32[24,12,8,1]{3,2,1,0:T(8,128)}, u32[]{:S(2)}) copy-start(f32[24,12,8,1]{3,2,1,0:T(8,128)} %get-tuple-element.41) | copy-start | bytes 27652
  20.7 5.6 %copy-start.5 = (f32[24,8,128]{2,0,1:T(8,128)}, f32[24,8,128]{2,0,1:T(8,128)S(1)}, u32[]{:S(2)}) copy-start(f32[24,8,128]{2,0,1:T(8,128)S(1)} %get-tuple-element.47) | copy-start | bytes 294916
  20.7 5.6 %copy-start.6 = (f32[24,8,128]{2,0,1:T(8,128)}, f32[24,8,128]{2,0,1:T(8,128)S(1)}, u32[]{:S(2)}) copy-start(f32[24,8,128]{2,0,1:T(8,128)S(1)} %get-tuple-element.48) | copy-start | bytes 294916
  21.1 5.2 %copy-start.14 = (pred[12]{0:T(512)(128)(4,1)}, pred[12]{0:T(512)(128)(4,1)S(1)}, u32[]{:S(2)}) copy-start(pred[12]{0:T(512)(128)(4,1)S(1)} %get-tuple-element.53) | copy-start | bytes 40
  21.1 5.2 %copy-start.15 = (pred[12]{0:T(512)(128)(4,1)}, pred[12]{0:T(512)(128)(4,1)S(1)}, u32[]{:S(2)}) copy-start(pred[12]{0:T(512)(128)(4,1)S(1)} %get-tuple-element.54) | copy-start | bytes 40
  21.8 4.5 %copy-start.3 = (f32[24,12,1,128]{3,0,1,2:T(8,128)S(1)}, f32[24,12,1,128]{3,0,1,2:T(8,128)}, u32[]{:S(2)}) copy-start(f32[24,12,1,128]{3,0,1,2:T(8,128)} %get-tuple-element.34) | copy-start | bytes 442372
  21.8 4.5 %copy-start.4 = (f32[24,12,1,128]{3,0,1,2:T(8,128)S(1)}, f32[24,12,1,128]{3,0,1,2:T(8,128)}, u32[]{:S(2)}) copy-start(f32[24,12,1,128]{3,0,1,2:T(8,128)} %get-tuple-element.35) | copy-start | bytes 442372
  37.3 10.2 %copy-start.2 = (f32[24,12,8,1]{3,0,1,2:T(8,128)}, f32[24,12,8,1]{3,0,1,2:T(8,128)S(1)}, u32[]{:S(2)}) copy-start(f32[24,12,8,1]{3,0,1,2:T(8,128)S(1)} %get-tuple-element.28) | copy-start | bytes 27652
  38.7 9.3 %collective-permute-start.6 = (f32[24,12,8]{0,1,2:T(8,128)}, f32[24,12,8]{0,1,2:T(8,128)}, u32[]{:S(2)}, u32[]{:S(2)}) collective-permute-start(f32[24,12,8]{0,1,2:T(8,128)} %bitcast.70), channel_id=1, source_target_pairs={{1,0},{2,1},{3,2},{4,3},{5,4},{6,5},{7,6},{0,7},{9,8},{10,9},{11,1... | collective-permute-start | bytes 27656 | tf_op jit(solution)/shard_map/ppermute | solution.py:20
  41.3 9.8 %collective-permute-start.4 = (f32[24,12,128]{2,0,1:T(8,128)}, f32[24,12,128]{2,0,1:T(8,128)}, u32[]{:S(2)}, u32[]{:S(2)}) collective-permute-start(f32[24,12,128]{2,0,1:T(8,128)} %get-tuple-element.19), channel_id=1, source_target_pairs={{8,0},{16,8},{24,16},{32,24},{40,32},{48,40},{56,48},{64,56},{72,6... | collective-permute-start | bytes 442376 | tf_op jit(solution)/shard_map/ppermute | solution.py:20
  46.1 7.6 %collective-permute-start.5 = (f32[24,12,128]{2,0,1:T(8,128)}, f32[24,12,128]{2,0,1:T(8,128)}, u32[]{:S(2)}, u32[]{:S(2)}) collective-permute-start(f32[24,12,128]{2,0,1:T(8,128)} %get-tuple-element.20), channel_id=1, source_target_pairs={{248,0},{0,8},{8,16},{16,24},{24,32},{32,40},{40,48},{48,56},{56,6... | collective-permute-start | bytes 442376 | tf_op jit(solution)/shard_map/ppermute | solution.py:20
  47.5 3.3 %collective-permute-start.7 = (f32[24,12,8]{0,1,2:T(8,128)}, f32[24,12,8]{0,1,2:T(8,128)S(1)}, u32[]{:S(2)}, u32[]{:S(2)}) collective-permute-start(f32[24,12,8]{0,1,2:T(8,128)} %bitcast.73), channel_id=1, source_target_pairs={{7,0},{0,1},{1,2},{2,3},{3,4},{4,5},{5,6},{6,7},{15,8},{8,9},{9,10... | collective-permute-start | bytes 27656 | tf_op jit(solution)/shard_map/ppermute | solution.py:20
  67.4 9.9 %collective-permute-start.10 = (f32[24,12,8]{0,1,2:T(8,128)}, f32[24,12,8]{0,1,2:T(8,128)}, u32[]{:S(2)}, u32[]{:S(2)}) collective-permute-start(f32[24,12,8]{0,1,2:T(8,128)} %bitcast.71), channel_id=1, source_target_pairs={{1,0},{2,1},{3,2},{4,3},{5,4},{6,5},{7,6},{0,7},{9,8},{10,9},{11,1... | collective-permute-start | bytes 27656 | tf_op jit(solution)/shard_map/ppermute | solution.py:20
  71.6 7.9 %collective-permute-start.8 = (f32[24,12,128]{2,0,1:T(8,128)}, f32[24,12,128]{2,0,1:T(8,128)}, u32[]{:S(2)}, u32[]{:S(2)}) collective-permute-start(f32[24,12,128]{2,0,1:T(8,128)} %get-tuple-element.5), channel_id=1, source_target_pairs={{8,0},{16,8},{24,16},{32,24},{40,32},{48,40},{56,48},{64,56},{72,6... | collective-permute-start | bytes 442376 | tf_op jit(solution)/shard_map/ppermute | solution.py:20
  75.9 8.8 %collective-permute-start.9 = (f32[24,12,128]{2,0,1:T(8,128)}, f32[24,12,128]{2,0,1:T(8,128)}, u32[]{:S(2)}, u32[]{:S(2)}) collective-permute-start(f32[24,12,128]{2,0,1:T(8,128)} %get-tuple-element.6), channel_id=1, source_target_pairs={{248,0},{0,8},{8,16},{16,24},{24,32},{32,40},{40,48},{48,56},{56,6... | collective-permute-start | bytes 442376 | tf_op jit(solution)/shard_map/ppermute | solution.py:20
  77.3 1.7 %collective-permute-start.11 = (f32[24,12,8]{0,1,2:T(8,128)}, f32[24,12,8]{0,1,2:T(8,128)S(1)}, u32[]{:S(2)}, u32[]{:S(2)}) collective-permute-start(f32[24,12,8]{0,1,2:T(8,128)} %bitcast.72), channel_id=1, source_target_pairs={{7,0},{0,1},{1,2},{2,3},{3,4},{4,5},{5,6},{6,7},{15,8},{8,9},{9,10... | collective-permute-start | bytes 27656 | tf_op jit(solution)/shard_map/ppermute | solution.py:20
where the time goes:
time: 92.8 us; the launch traced here: 92.3 us
  local copies, waits for them, and re-layouts  32.5 us (35%)
  starting transfers between devices  25.6 us (28%)
  other arithmetic  14.7 us (16%)
  matrix products  10.9 us (12%)
  waiting for transfers between devices  8.13 us (9%)
    ppermute x12, starting transfers between devices, shifted(): return lax.ppermute(block, axis, route)  25.6 us
    sub x3, other arithmetic, advance(): total - field * field  14.6 us
    dot_general x12, matrix products, reorder(): jnp.einsum('st,tzc->szc', select, rim, precision=lax.Precision.HIGHEST)  10.9 us
    ppermute x12, waiting for transfers between devices, shifted(): return lax.ppermute(block, axis, route)  8.13 us
    unnamed x35, local copies, waits for them, and re-layouts  7.11 us
    slice x6, local copies, waits for them, and re-layouts, advance(): jnp.roll(field, 1, axis=1)  4.55 us
    slice x3, local copies, waits for them, and re-layouts, advance(): jnp.roll(field, 1, axis=3)  3.98 us
    slice x3, local copies, waits for them, and re-layouts, advance(): jnp.roll(field, 1, axis=2)  3.29 us
  transfers between devices with their start and end apart: 12, of which 5 were waited for; matrix products, arithmetic and copies ran while one was open for 21% of the time, Pallas kernels for 0%

commit v1 on v0

v1 whole, which is shorter than its diff:
```python
import functools

import jax
import jax.numpy as jnp
from jax import lax
from jax.experimental import pallas as pl
from jax.experimental.pallas import tpu as pltpu
from jax.sharding import PartitionSpec as P

STEPS = 3
SHARED = 6
FACES = 4
MESH = pl.DeviceIdType.MESH

SELF = 0.45
TOTAL = 0.15
LINK = 0.1


def kernel(slots, depth, nx, ny, tab, planes, start, out, field, local, halo, send_x, recv_x, send_y, recv_y,
           in_sem, send_sem, recv_sem):
    rows, cols = 8, 128
    i, j = lax.axis_index("gx"), lax.axis_index("gy")
    across = (
        (lax.rem(i + nx - 1, nx), j),
        (lax.rem(i + 1, nx), j),
        (i, lax.rem(j + ny - 1, ny)),
        (i, lax.rem(j + 1, ny)),
    )
    barrier = pltpu.get_barrier_semaphore()
    for device in across:
        pl.semaphore_signal(barrier, inc=1, device_id=device, device_id_type=MESH)
    load = pltpu.make_async_copy(start, field, in_sem)
    load.start()

    row = lax.broadcasted_iota(jnp.int32, (rows, cols), 0)
    col = lax.broadcasted_iota(jnp.int32, (rows, cols), 1)
    zero = jnp.zeros((rows, cols), jnp.float32)

    def tile(slot, layer):
        return slot * depth + layer

    def clear(slot, carry):
        for layer in range(depth):
            halo[tile(slot, layer)] = zero
        return carry

    lax.fori_loop(0, slots + 1, clear, 0)

    def copy(step, face):
        source, target = (send_x, recv_x) if face < 2 else (send_y, recv_y)
        lane = face % 2
        return pltpu.make_async_remote_copy(
            src_ref=source.at[step, lane],
            dst_ref=target.at[step, 1 - lane],
            send_sem=send_sem.at[step, face],
            recv_sem=recv_sem.at[step, face ^ 1],
            device_id=across[face],
            device_id_type=MESH,
        )

    def arrival(step, face):
        target = recv_x if face < 2 else recv_y
        return pltpu.make_async_remote_copy(
            src_ref=target.at[step, face % 2],
            dst_ref=target.at[step, face % 2],
            send_sem=send_sem.at[step, face],
            recv_sem=recv_sem.at[step, face],
            device_id=across[face],
            device_id_type=MESH,
        )

    def pack_x(step, source):
        for face in range(2):
            edge = 0 if face == 0 else rows - 1
            for k in range(SHARED):
                slot = tab[32 + face * SHARED + k]
                for layer in range(depth):
                    rim = source[tile(slot, layer), edge : edge + 1]
                    if step:
                        rim = rim + LINK * recv_x[step - 1, face, k, layer : layer + 1]
                    send_x[step, face, k, layer : layer + 1] = rim

    def pack_y(step, source):
        for face in range(2, 4):
            edge = 0 if face == 2 else cols - 1
            packed = zero
            for k in range(SHARED):
                slot = tab[32 + face * SHARED + k]
                for layer in range(depth):
                    place = k * depth + layer
                    moved = pltpu.roll(source[tile(slot, layer)], (place - edge) % cols, 1)
                    packed = jnp.where(col == place, moved, packed)
            if step:
                packed = packed + LINK * recv_y[step - 1, face - 2]
            send_y[step, face - 2] = packed

    def unpack(step):
        for face in range(2):
            edge = 0 if face == 0 else rows - 1
            for k in range(SHARED):
                for layer in range(depth):
                    at = tile(face * SHARED + k, layer)
                    halo[at, edge : edge + 1] = LINK * recv_x[step, face, k, layer : layer + 1]
        for face in range(2, 4):
            edge = 0 if face == 2 else cols - 1
            packed = LINK * recv_y[step, face - 2]
            for k in range(SHARED):
                for layer in range(depth):
                    place = k * depth + layer
                    moved = pltpu.roll(packed, (edge - place) % cols, 1)
                    halo[tile(face * SHARED + k, layer)] = jnp.where(col == edge, moved, 0.0)

    def totals(step):
        def body(slot, sums):
            held = tab[slot]
            out_sums = []
            for layer in range(depth):
                at = tile(slot, layer)
                value = field[at] if step == 0 else local[at] + halo[tile(held, layer)]
                if step:
                    field[at] = value
                out_sums.append(sums[layer] + value * value)
            return tuple(out_sums)

        return lax.fori_loop(0, slots, body, (zero,) * depth)

    def update(sums):
        coefs = tuple(SELF - TOTAL * s for s in sums)
        below, above = planes[0], planes[1]

        def body(slot, carry):
            grain = tab[64 + slot]
            values = [field[tile(slot, layer)] for layer in range(depth)]
            small = [LINK * v for v in values]
            low = jnp.where(below == grain, LINK, 0.0)
            high = jnp.where(above == grain, LINK, 0.0)
            for layer in range(depth):
                v, w = values[layer], small[layer]
                near = (
                    jnp.where(row == rows - 1, 0.0, pltpu.roll(w, rows - 1, 0))
                    + jnp.where(row == 0, 0.0, pltpu.roll(w, 1, 0))
                    + jnp.where(col == cols - 1, 0.0, pltpu.roll(w, cols - 1, 1))
                    + jnp.where(col == 0, 0.0, pltpu.roll(w, 1, 1))
                    + (small[layer - 1] if layer else low)
                    + (small[layer + 1] if layer < depth - 1 else high)
                )
                local[tile(slot, layer)] = v * (coefs[layer] + v * w) + near
            return carry

        lax.fori_loop(0, slots, body, 0)

    load.wait()
    pack_x(0, field)
    pl.semaphore_wait(barrier, FACES)
    for step in range(STEPS):
        if step:
            for face in range(FACES):
                arrival(step - 1, face).wait_recv()
            pack_x(step, local)
        copy(step, 0).start()
        copy(step, 1).start()
        pack_y(step, local if step else field)
        copy(step, 2).start()
        copy(step, 3).start()
        if step:
            unpack(step - 1)
        update(totals(step))
    for face in range(FACES):
        arrival(STEPS - 1, face).wait_recv()
    unpack(STEPS - 1)

    def finish(slot, carry):
        held = tab[slot]
        for layer in range(depth):
            at = tile(slot, layer)
            out[at] = local[at] + halo[tile(held, layer)]
        return carry

    lax.fori_loop(0, slots, finish, 0)
    for step in range(STEPS):
        for face in range(FACES):
            copy(step, face).wait_send()


def tables(grain_ids, channel_maps):
    slots = grain_ids.shape[-1]
    maps = channel_maps[0, 0]
    own = jnp.arange(slots, dtype=jnp.int32)
    upper = (jnp.arange(FACES, dtype=jnp.int32) % 2 == 1)[:, None]
    linked = maps >= 0
    key = jnp.where(linked, jnp.where(upper, own[None, :], maps), slots)
    rank = jnp.sum((key[:, None, :] < key[:, :, None]).astype(jnp.int32), axis=2)
    pair = jnp.arange(FACES, dtype=jnp.int32)[:, None] * SHARED + rank
    held = jnp.min(jnp.where(linked, pair, FACES * SHARED), axis=0)
    places = jnp.arange(FACES * SHARED, dtype=jnp.int32)
    source = jnp.sum(jnp.where(held[None, :] == places[:, None], own[None, :], 0), axis=1)
    grains = jnp.where(grain_ids[0, 0] >= 0, grain_ids[0, 0], -1)
    pad = lambda x: jnp.pad(x, (0, 32 - slots))
    return jnp.concatenate([pad(held), pad(source), pad(grains)]).astype(jnp.int32)


def solution(mesh):
    nx, ny = mesh.shape["gx"], mesh.shape["gy"]

    def on_device(order_params, grain_ids, channel_maps, zplanes):
        slots, depth, rows, cols = order_params.shape
        tiles = (slots * depth, rows, cols)
        tab = tables(grain_ids, channel_maps)
        result = pl.pallas_call(
            functools.partial(kernel, slots, depth, nx, ny),
            out_shape=jax.ShapeDtypeStruct(tiles, jnp.float32),
            in_specs=[
                pl.BlockSpec(memory_space=pltpu.SMEM),
                pl.BlockSpec(memory_space=pltpu.VMEM),
                pl.BlockSpec(memory_space=pl.ANY),
            ],
            out_specs=pl.BlockSpec(memory_space=pltpu.VMEM),
            scratch_shapes=[
                pltpu.VMEM(tiles, jnp.float32),
                pltpu.VMEM(tiles, jnp.float32),
                pltpu.VMEM(((slots + 1) * depth, rows, cols), jnp.float32),
                pltpu.VMEM((STEPS, 2, SHARED, depth, cols), jnp.float32),
                pltpu.VMEM((STEPS, 2, SHARED, depth, cols), jnp.float32),
                pltpu.VMEM((STEPS, 2, rows, cols), jnp.float32),
                pltpu.VMEM((STEPS, 2, rows, cols), jnp.float32),
                pltpu.SemaphoreType.DMA,
                pltpu.SemaphoreType.DMA((STEPS, FACES)),
                pltpu.SemaphoreType.DMA((STEPS, FACES)),
            ],
            compiler_params=pltpu.CompilerParams(
                collective_id=0, has_side_effects=True, vmem_limit_bytes=16 * 2**20
            ),
        )(tab, zplanes, order_params.reshape(tiles))
        return result.reshape(order_params.shape)

    in_specs = (
        P(None, None, "gx", "gy"),
        P("gx", "gy", None),
        P("gx", "gy", None, None),
        P(None, "gx", "gy"),
    )
    return jax.shard_map(
        on_device, mesh=mesh, in_specs=in_specs, out_specs=P(None, None, "gx", "gy"), check_vma=False
    )
```

time: 92.8 us -> 29.1 us (0.31)
  local copies, waits for them, and re-layouts: 32.5 us -> 2.99 us
  starting transfers between devices: 25.6 us -> 0 us
  Pallas kernels: 0 us -> 23.3 us
  other arithmetic: 14.7 us -> 2.6 us
  matrix products: 10.9 us -> 0 us
  waiting for transfers between devices: 8.13 us -> 0 us
    ppermute x12 -> x0, starting transfers between devices: 25.6 us -> none  [shifted(): return lax.ppermute(block, axis, route)]
    pallas_call x0 -> x1, Pallas kernels: none -> 23.3 us  [on_device(): pl.pallas_call(functools.partial(kernel, slots, depth, nx, ny), out_shape...]
    slice x17 -> x0, local copies, waits for them, and re-layouts: 15.4 us -> none  [the longest x6 4.55 us: advance(): jnp.roll(field, 1, axis=1)]
    sub x3 -> x0, other arithmetic: 14.6 us -> none  [advance(): total - field * field]
    dot_general x12 -> x0, matrix products: 10.9 us -> none  [reorder(): jnp.einsum('st,tzc->szc', select, rim, precision=lax.Precision.HIGHEST)]
    squeeze x7 -> x0, local copies, waits for them, and re-layouts: 8.3 us -> none  [the longest x2 2.87 us: on_device(): lower_y = reorder(shifted(field[:, :, :, -1], 'gy', 1), face_maps[2])]
    ppermute x12 -> x0, waiting for transfers between devices: 8.13 us -> none  [shifted(): return lax.ppermute(block, axis, route)]
    unnamed x35 -> x5, local copies, waits for them, and re-layouts: 7.11 us -> 2.99 us
  transfers between devices with their start and end apart: 12 -> 0, of which waited for: 5 -> 0; matrix products, arithmetic and copies ran while one was open for 21% -> 0% of each run, Pallas kernels for 0% -> 0%
where the time goes in v1:
time: 29.1 us; the launch traced here: 28.9 us
  Pallas kernels  23.3 us (80%)
  local copies, waits for them, and re-layouts  2.99 us (10%)
  other arithmetic  2.6 us (9%)
    pallas_call x1, Pallas kernels, on_device(): pl.pallas_call(functools.partial(kernel, slots, depth, nx, ny), out_shape...  23.3 us
    unnamed x5, local copies, waits for them, and re-layouts  2.99 us
    reduce_min x1, other arithmetic, tables(): held = jnp.min(jnp.where(linked, pair, FACES * SHARED), axis=0)  0.78 us
    select_n x1, other arithmetic, tables(): key = jnp.where(linked, jnp.where(upper, own[None, :], maps), slots)  0.76 us
    select_n x1, other arithmetic, tables(): grains = jnp.where(grain_ids[0, 0] >= 0, grain_ids[0, 0], -1)  0.66 us

profile of v1, /device:TPU:1, one launch (start us, length us, event | category | flops | bytes accessed | tf_op | source)
XLA Modules:
  0.0 28.9 jit_solution(12575128441437194270)
XLA Ops:
  0.0 0.7 %compare_select_fusion = s32[24]{0:T(128)S(1)} fusion(s32[1,1,24]{2,1,0:T(1,128)} %param.5), kind=kLoop, calls=%fused_computation.3 | loop fusion | flops 48 | bytes 192 | tf_op jit(solution)/shard_map/jit(_where)/select_n | solution.py:198
  0.7 0.8 %fusion = s32[4,24]{1,0:T(4,128)S(1)} fusion(s32[1,1,4,24]{3,2,1,0:T(4,128)} %param.6, pred[4]{0:T(512)(128)(4,1)S(1)} %fusion.1), kind=kLoop, calls=%fused_computation.6 | loop fusion | flops 288 | bytes 772 | tf_op jit(solution)/shard_map/jit(_where)/select_n | solution.py:192
  1.4 0.2 convert_reduce_fusion
  1.6 0.8 %select_reduce_fusion.1 = s32[24]{0:T(128)S(1)} fusion(s32[4,24]{1,0:T(4,128)S(1)} %convert_reduce_fusion, s32[4]{0:T(128)S(1)} %iota_multiply_fusion, s32[1,1,4,24]{3,2,1,0:T(4,128)} %param.6), kind=kLoop, calls=%fused_computation.7 | loop fusion | flops 360 | bytes 880 | tf_op jit(solution)/shard_map/reduce_min | solution.py:195
  2.4 0.1 select_reduce_fusion
  2.5 0.1 pad_add_fusion.tab
  2.6 0.0 copy-start
  2.6 1.3 %copy-done = f32[24,12,8,128]{3,2,1,0:T(8,128)S(1)} copy-done((f32[24,12,8,128]{3,2,1,0:T(8,128)S(1)}, f32[24,12,8,128]{3,2,1,0:T(8,128)}, u32[]{:S(2)}) %copy-start) | copy-done | bytes 1179672
  3.9 0.0 copy-start.1
  3.9 0.7 %copy-done.1 = s32[2,8,128]{2,1,0:T(8,128)S(1)} copy-done((s32[2,8,128]{2,1,0:T(8,128)S(1)}, s32[2,8,128]{2,1,0:T(8,128)}, u32[]{:S(2)}) %copy-start.1) | copy-done | bytes 8216
  4.6 23.3 %shard_map.46 = f32[288,8,128]{2,1,0:T(8,128)S(1)} custom-call(s32[96]{0:T(128)S(1)} %pad_add_fusion.tab, s32[2,8,128]{2,1,0:T(8,128)S(1)} %copy-done.1, f32[288,8,128]{2,1,0:T(8,128)S(1)} %bitcast.14), custom_call_target="tpu_custom_call" | custom-call | tf_op jit(solution)/shard_map/pallas_call | solution.py:210
  27.9 1.0 %copy.6 = f32[24,12,8,128]{3,2,1,0:T(8,128)} copy(f32[24,12,8,128]{3,2,1,0:T(8,128)S(1)} %bitcast.13) | data formatting | bytes 2359296
  (2 shorter events, 0.0 us)
Async XLA Ops:
  2.6 1.3 %copy-start = (f32[24,12,8,128]{3,2,1,0:T(8,128)S(1)}, f32[24,12,8,128]{3,2,1,0:T(8,128)}, u32[]{:S(2)}) copy-start(f32[24,12,8,128]{3,2,1,0:T(8,128)} %param.4) | copy-start | bytes 3538948
  3.9 0.7 %copy-start.1 = (s32[2,8,128]{2,1,0:T(8,128)S(1)}, s32[2,8,128]{2,1,0:T(8,128)}, u32[]{:S(2)}) copy-start(s32[2,8,128]{2,1,0:T(8,128)} %planes.1) | copy-start | bytes 24580

commit v2 on v1

v2 whole, which is shorter than its diff:
```python
import functools

import jax
import jax.numpy as jnp
from jax import lax
from jax.experimental import pallas as pl
from jax.experimental.pallas import tpu as pltpu
from jax.sharding import PartitionSpec as P

SHARED = 6
FACES = 4
MESH = pl.DeviceIdType.MESH

SELF = 0.45
TOTAL = 0.15
LINK = 0.1

RIM, LOCAL, SUMS = 0, 1, 2


def kernel(slots, depth, nx, ny, maps_in, grains_in, planes_in, start, out, field, local, halo, maps, key_box, table, tab,
           grains, planes, rim_x, got_rim_x, loc_x, got_loc_x, sum_x, got_sum_x, rim_y, got_rim_y, loc_y, got_loc_y, sum_y,
           got_sum_y, next_x, next_y, load_sem, send_sem, recv_sem):
    rows, cols = 8, 128
    i, j = lax.axis_index("gx"), lax.axis_index("gy")
    across = (
        (lax.rem(i + nx - 1, nx), j),
        (lax.rem(i + 1, nx), j),
        (i, lax.rem(j + ny - 1, ny)),
        (i, lax.rem(j + 1, ny)),
    )
    barrier = pltpu.get_barrier_semaphore()
    for device in across:
        pl.semaphore_signal(barrier, inc=1, device_id=device, device_id_type=MESH)
    loads = [
        pltpu.make_async_copy(maps_in, maps, load_sem.at[0]),
        pltpu.make_async_copy(start, field, load_sem.at[1]),
        pltpu.make_async_copy(grains_in, grains, load_sem.at[2]),
        pltpu.make_async_copy(planes_in, planes, load_sem.at[3]),
    ]
    for load in loads:
        load.start()

    row = lax.broadcasted_iota(jnp.int32, (rows, cols), 0)
    col = lax.broadcasted_iota(jnp.int32, (rows, cols), 1)
    zero = jnp.zeros((rows, cols), jnp.float32)

    def tile(slot, layer):
        return slot * depth + layer

    def clear(slot, carry):
        for layer in range(depth):
            halo[tile(slot, layer)] = zero
        return carry

    lax.fori_loop(0, slots + 1, clear, 0)

    loads[0].wait()
    key_box[...] = jnp.full((rows, cols), -1, jnp.int32)
    key_box[0:FACES, 0:slots] = maps[...]
    entries = key_box[...]
    linked = entries >= 0
    upper = (row == 1) | (row == 3)
    key = jnp.where(linked, jnp.where(upper, col, entries), slots)
    rank = jnp.zeros((rows, cols), jnp.int32)
    for slot in range(slots):
        rank = rank + jnp.where(key[:, slot : slot + 1] < key, 1, 0)
    pair = jnp.where(linked & (rank < SHARED), row * SHARED + rank, FACES * SHARED)
    held = jnp.broadcast_to(jnp.min(pair, axis=0, keepdims=True), (rows, cols))
    source = jnp.zeros((rows, cols), jnp.int32)
    for slot in range(slots):
        source = jnp.maximum(source, jnp.where(held[:, slot : slot + 1] == col, slot, 0))
    table[...] = jnp.where(row == 0, held, source)
    fetch = pltpu.make_async_copy(table, tab, load_sem.at[4])
    fetch.start()

    buffers = {
        RIM: ((rim_x, got_rim_x), (rim_y, got_rim_y)),
        LOCAL: ((loc_x, got_loc_x), (loc_y, got_loc_y)),
        SUMS: ((sum_x, got_sum_x), (sum_y, got_sum_y)),
    }

    def copy(kind, face):
        sent, got = buffers[kind][face // 2]
        return pltpu.make_async_remote_copy(
            src_ref=sent.at[face % 2],
            dst_ref=got.at[1 - face % 2],
            send_sem=send_sem.at[kind, face],
            recv_sem=recv_sem.at[kind, face ^ 1],
            device_id=across[face],
            device_id_type=MESH,
        )

    def wait_for(kind, face):
        copy(kind, face ^ 1).wait_recv()

    def pair_slot(face, k):
        return tab[1, face * SHARED + k]

    def gather_columns(face, column, tiles):
        packed = zero
        for k in range(SHARED):
            slot = pair_slot(face, k)
            for layer in range(depth):
                place = k * depth + layer
                moved = pltpu.roll(tiles[tile(slot, layer)], (place - column) % cols, 1)
                packed = jnp.where(col == place, moved, packed)
        return packed

    def scatter(face, layer_row, packed):
        edge = 0 if face % 2 == 0 else (rows if face < 2 else cols) - 1
        for k in range(SHARED):
            for layer in range(depth):
                at = tile(face * SHARED + k, layer)
                if face < 2:
                    halo[at, edge : edge + 1] = LINK * layer_row(layer, k)
                else:
                    moved = pltpu.roll(packed, (edge - (k * depth + layer)) % cols, 1)
                    halo[at] = jnp.where(col == edge, moved, 0.0)

    def totals(first):
        def body(slot, sums):
            held_pair = tab[0, slot]
            out_sums = []
            for layer in range(depth):
                at = tile(slot, layer)
                value = field[at] if first else local[at] + halo[tile(held_pair, layer)]
                if not first:
                    field[at] = value
                out_sums.append(sums[layer] + value * value)
            return tuple(out_sums)

        return lax.fori_loop(0, slots, body, (zero,) * depth)

    def update(sums):
        coefs = tuple(SELF - TOTAL * s for s in sums)
        below, above = planes[0], planes[1]

        def body(slot, carry):
            grain = grains[slot]
            grain = jnp.where(grain >= 0, grain, -1)
            values = [field[tile(slot, layer)] for layer in range(depth)]
            small = [LINK * v for v in values]
            low = jnp.where(below == grain, LINK, 0.0)
            high = jnp.where(above == grain, LINK, 0.0)
            for layer in range(depth):
                v, w = values[layer], small[layer]
                near = (
                    jnp.where(row == rows - 1, 0.0, pltpu.roll(w, rows - 1, 0))
                    + jnp.where(row == 0, 0.0, pltpu.roll(w, 1, 0))
                    + jnp.where(col == cols - 1, 0.0, pltpu.roll(w, cols - 1, 1))
                    + jnp.where(col == 0, 0.0, pltpu.roll(w, 1, 1))
                    + (small[layer - 1] if layer else low)
                    + (small[layer + 1] if layer < depth - 1 else high)
                )
                local[tile(slot, layer)] = v * (coefs[layer] + v * w) + near
            return carry

        lax.fori_loop(0, slots, body, 0)

    loads[1].wait()
    sums = totals(True)
    fetch.wait()
    for face in range(2):
        edge = 0 if face == 0 else rows - 1
        for k in range(SHARED):
            slot = pair_slot(face, k)
            for layer in range(depth):
                rim_x[face, layer, k : k + 1] = field[tile(slot, layer), edge : edge + 1]
    for face in range(2, 4):
        rim_y[face - 2] = gather_columns(face, 0 if face == 2 else cols - 1, field)
    pl.semaphore_wait(barrier, FACES)
    for face in range(FACES):
        copy(RIM, face).start()

    loads[2].wait()
    loads[3].wait()
    update(sums)

    for face in range(2):
        edge, second = (0, 1) if face == 0 else (rows - 1, rows - 2)
        for k in range(SHARED):
            slot = pair_slot(face, k)
            grain = grains[slot]
            grain = jnp.where(grain >= 0, grain, -1)
            for layer in range(depth):
                at = tile(slot, layer)
                loc_x[face, 0, layer, k : k + 1] = local[at, edge : edge + 1]
                behind = local[at, second : second + 1]
                if layer == 0:
                    behind = behind + jnp.where(planes[0, edge : edge + 1] == grain, 1.0, 0.0)
                if layer == depth - 1:
                    behind = behind + jnp.where(planes[1, edge : edge + 1] == grain, 1.0, 0.0)
                loc_x[face, 1, layer, k : k + 1] = behind
    for face in range(2, 4):
        edge, second = (0, 1) if face == 2 else (cols - 1, cols - 2)
        loc_y[face - 2, 0] = gather_columns(face, edge, local)
        behind = gather_columns(face, second, local)
        for k in range(SHARED):
            grain = grains[pair_slot(face, k)]
            grain = jnp.where(grain >= 0, grain, -1)
            for plane, layer in ((0, 0), (1, depth - 1)):
                place = k * depth + layer
                frozen = jnp.where(planes[plane] == grain, 1.0, 0.0)
                moved = pltpu.roll(frozen, (place - edge) % cols, 1)
                behind = behind + jnp.where(col == place, moved, 0.0)
        loc_y[face - 2, 1] = behind
    for face in range(FACES):
        copy(LOCAL, face).start()

    for face in range(FACES):
        wait_for(RIM, face)
        if face < 2:
            scatter(face, lambda layer, k: got_rim_x[face, layer, k : k + 1], None)
        else:
            scatter(face, None, LINK * got_rim_y[face - 2])
    sums = totals(False)

    for face in range(2):
        edge = 0 if face == 0 else rows - 1
        for layer in range(depth):
            sum_x[face, layer : layer + 1] = sums[layer][edge : edge + 1]
    for face in range(2, 4):
        edge = 0 if face == 2 else cols - 1
        packed = zero
        for layer in range(depth):
            packed = jnp.where(col == layer, pltpu.roll(sums[layer], (layer - edge) % cols, 1), packed)
        two = packed + pltpu.roll(packed, depth, 1)
        four = two + pltpu.roll(two, 2 * depth, 1)
        sum_y[face - 2] = four + pltpu.roll(two, 4 * depth, 1)
    for face in range(FACES):
        copy(SUMS, face).start()

    update(sums)

    for face in range(FACES):
        wait_for(LOCAL, face)
        if face < 2:
            for layer in range(depth):
                next_x[face, layer] = got_loc_x[face, 0, layer] + LINK * rim_x[face, layer]
            scatter(face, lambda layer, k: next_x[face, layer, k : k + 1], None)
        else:
            next_y[face - 2] = got_loc_y[face - 2, 0] + LINK * rim_y[face - 2]
            scatter(face, None, LINK * next_y[face - 2])
    update(totals(False))

    group = lax.rem(col, depth)
    lane = col[:SHARED]
    for face in range(FACES):
        wait_for(SUMS, face)
        if face < 2:
            rims = [next_x[face, layer] for layer in range(depth)]
            for layer in range(depth):
                r = rims[layer]
                near = (
                    got_loc_x[face, 1, layer]
                    + loc_x[face, 0, layer]
                    + LINK * got_rim_x[face, layer]
                    + jnp.where(lane == cols - 1, 0.0, pltpu.roll(r, cols - 1, 1))
                    + jnp.where(lane == 0, 0.0, pltpu.roll(r, 1, 1))
                )
                if layer:
                    near = near + rims[layer - 1]
                if layer < depth - 1:
                    near = near + rims[layer + 1]
                total = jnp.broadcast_to(got_sum_x[face, layer : layer + 1], r.shape)
                next_x[face, layer] = r * (SELF - TOTAL * total + LINK * r * r) + LINK * near
            scatter(face, lambda layer, k: next_x[face, layer, k : k + 1], None)
        else:
            r = next_y[face - 2]
            near = (
                got_loc_y[face - 2, 1]
                + loc_y[face - 2, 0]
                + LINK * got_rim_y[face - 2]
                + jnp.where(row == rows - 1, 0.0, pltpu.roll(r, rows - 1, 0))
                + jnp.where(row == 0, 0.0, pltpu.roll(r, 1, 0))
                + jnp.where(group == depth - 1, 0.0, pltpu.roll(r, cols - 1, 1))
                + jnp.where(group == 0, 0.0, pltpu.roll(r, 1, 1))
            )
            total = got_sum_y[face - 2]
            scatter(face, None, LINK * (r * (SELF - TOTAL * total + LINK * r * r) + LINK * near))

    def finish(slot, carry):
        held_pair = tab[0, slot]
        for layer in range(depth):
            at = tile(slot, layer)
            out[at] = local[at] + halo[tile(held_pair, layer)]
        return carry

    lax.fori_loop(0, slots, finish, 0)
    for kind in (RIM, LOCAL, SUMS):
        for face in range(FACES):
            copy(kind, face).wait_send()


def solution(mesh):
    nx, ny = mesh.shape["gx"], mesh.shape["gy"]

    def on_device(order_params, grain_ids, channel_maps, zplanes):
        slots, depth, rows, cols = order_params.shape
        tiles = (slots * depth, rows, cols)
        rim_x = pltpu.VMEM((2, depth, SHARED, cols), jnp.float32)
        loc_x = pltpu.VMEM((2, 2, depth, SHARED, cols), jnp.float32)
        sum_x = pltpu.VMEM((2, depth, cols), jnp.float32)
        rim_y = pltpu.VMEM((2, rows, cols), jnp.float32)
        loc_y = pltpu.VMEM((2, 2, rows, cols), jnp.float32)
        operands = (channel_maps.reshape(FACES, slots), grain_ids.reshape(slots), zplanes, order_params.reshape(tiles))
        result = pl.pallas_call(
            functools.partial(kernel, slots, depth, nx, ny),
            out_shape=jax.ShapeDtypeStruct(tiles, jnp.float32),
            in_specs=[pl.BlockSpec(memory_space=pltpu.HBM)] * 4,
            out_specs=pl.BlockSpec(memory_space=pltpu.VMEM),
            scratch_shapes=[
                pltpu.VMEM(tiles, jnp.float32),
                pltpu.VMEM(tiles, jnp.float32),
                pltpu.VMEM(((FACES * SHARED + 1) * depth, rows, cols), jnp.float32),
                pltpu.VMEM((FACES, slots), jnp.int32),
                pltpu.VMEM((rows, cols), jnp.int32),
                pltpu.VMEM((rows, cols), jnp.int32),
                pltpu.SMEM((rows, cols), jnp.int32),
                pltpu.SMEM((slots,), jnp.int32),
                pltpu.VMEM((2, rows, cols), jnp.int32),
                rim_x, rim_x, loc_x, loc_x, sum_x, sum_x,
                rim_y, rim_y, loc_y, loc_y, rim_y, rim_y,
                rim_x, rim_y,
                pltpu.SemaphoreType.DMA((5,)),
                pltpu.SemaphoreType.DMA((3, FACES)),
                pltpu.SemaphoreType.DMA((3, FACES)),
            ],
            compiler_params=pltpu.CompilerParams(
                collective_id=0, has_side_effects=True, vmem_limit_bytes=16 * 2**20
            ),
        )(*[pltpu.with_memory_space_constraint(x, pltpu.HBM) for x in operands])
        return result.reshape(order_params.shape)

    in_specs = (
        P(None, None, "gx", "gy"),
        P("gx", "gy", None),
        P("gx", "gy", None, None),
        P(None, "gx", "gy"),
    )
    return jax.shard_map(
        on_device, mesh=mesh, in_specs=in_specs, out_specs=P(None, None, "gx", "gy"), check_vma=False
    )
```

time: 29.1 us -> 20.9 us (0.72)
  Pallas kernels: 23.3 us -> 19.8 us
  other arithmetic: 2.6 us -> 0 us
  local copies, waits for them, and re-layouts: 2.99 us -> 1.02 us
    pallas_call x1, Pallas kernels: 23.3 us -> 19.8 us  [on_device(): pl.pallas_call(functools.partial(kernel, slots, depth, nx, ny), out_shape...]
    unnamed x5 -> x1, local copies, waits for them, and re-layouts: 2.99 us -> 1.02 us
    select_n x2 -> x0, other arithmetic: 1.41 us -> none  [the longest x1 0.76 us: tables(): key = jnp.where(linked, jnp.where(upper, own[None, :], maps), slots)]
    reduce_min x1 -> x0, other arithmetic: 0.78 us -> none  [tables(): held = jnp.min(jnp.where(linked, pair, FACES * SHARED), axis=0)]
    reduce_sum x2 -> x0, other arithmetic: 0.33 us -> none  [the longest x1 0.21 us: tables(): jnp.sum((key[:, None, :] < key[:, :, None]).astype(jnp.int32), axis=2)]
where the time goes in v2:
time: 20.9 us; the launch traced here: 20.8 us
  Pallas kernels  19.8 us (95%)
  local copies, waits for them, and re-layouts  1.02 us (5%)
    pallas_call x1, Pallas kernels, on_device(): pl.pallas_call(functools.partial(kernel, slots, depth, nx, ny), out_shape...  19.8 us
    unnamed x1, local copies, waits for them, and re-layouts  1.02 us

profile of v2, /device:TPU:1, one launch (start us, length us, event | category | flops | bytes accessed | tf_op | source)
XLA Modules:
  0.0 20.8 jit_solution(209087429606084509)
XLA Ops:
  0.0 19.8 %shard_map.46 = f32[288,8,128]{2,1,0:T(8,128)S(1)} custom-call(s32[4,24]{1,0:T(4,128)} %bitcast.6, s32[24]{0:T(128)} %bitcast.7, s32[2,8,128]{2,1,0:T(8,128)} %planes_in.1, f32[288,8,128]{2,1,0:T(8,128)} %bitcast.5), custom_call_target="tpu_custom_call" | custom-call | tf_op jit(solution)/shard_map/pallas_call | solution.py:308
  19.8 1.0 %copy.6 = f32[24,12,8,128]{3,2,1,0:T(8,128)} copy(f32[24,12,8,128]{3,2,1,0:T(8,128)S(1)} %bitcast.4) | data formatting | bytes 2359296

commit v3 on v2

--- a/solution.py
+++ b/solution.py
@@ -15,12 +15,13 @@
 TOTAL = 0.15
 LINK = 0.1
 
-RIM, LOCAL, SUMS = 0, 1, 2
+RIM, LOCAL, BEHIND, SUMS = 0, 1, 2, 3
+UNROLL = 8
 
 
 def kernel(slots, depth, nx, ny, maps_in, grains_in, planes_in, start, out, field, local, halo, maps, key_box, table, tab,
-           grains, planes, rim_x, got_rim_x, loc_x, got_loc_x, sum_x, got_sum_x, rim_y, got_rim_y, loc_y, got_loc_y, sum_y,
-           got_sum_y, next_x, next_y, load_sem, send_sem, recv_sem):
+           grains, planes, rim_x, got_rim_x, loc_x, got_loc_x, row_x, got_row_x, sum_x, got_sum_x, rim_y, got_rim_y, loc_y,
+           got_loc_y, row_y, got_row_y, sum_y, got_sum_y, next_x, next_y, load_sem, send_sem, recv_sem):
     rows, cols = 8, 128
     i, j = lax.axis_index("gx"), lax.axis_index("gy")
     across = (
@@ -34,7 +35,7 @@
         pl.semaphore_signal(barrier, inc=1, device_id=device, device_id_type=MESH)
     loads = [
         pltpu.make_async_copy(maps_in, maps, load_sem.at[0]),
-        pltpu.make_async_copy(start, field, load_sem.at[1]),
+        pltpu.make_async_copy(start, field.at[pl.ds(0, slots * depth)], load_sem.at[1]),
         pltpu.make_async_copy(grains_in, grains, load_sem.at[2]),
         pltpu.make_async_copy(planes_in, planes, load_sem.at[3]),
     ]
@@ -54,6 +55,9 @@
         return carry
 
     lax.fori_loop(0, slots + 1, clear, 0)
+    for layer in range(depth):
+        field[tile(slots, layer)] = zero
+        local[tile(slots, layer)] = zero
 
     loads[0].wait()
     key_box[...] = jnp.full((rows, cols), -1, jnp.int32)
@@ -67,9 +71,9 @@
         rank = rank + jnp.where(key[:, slot : slot + 1] < key, 1, 0)
     pair = jnp.where(linked & (rank < SHARED), row * SHARED + rank, FACES * SHARED)
     held = jnp.broadcast_to(jnp.min(pair, axis=0, keepdims=True), (rows, cols))
-    source = jnp.zeros((rows, cols), jnp.int32)
+    source = jnp.full((rows, cols), slots, jnp.int32)
     for slot in range(slots):
-        source = jnp.maximum(source, jnp.where(held[:, slot : slot + 1] == col, slot, 0))
+        source = jnp.minimum(source, jnp.where(held[:, slot : slot + 1] == col, slot, slots))
     table[...] = jnp.where(row == 0, held, source)
     fetch = pltpu.make_async_copy(table, tab, load_sem.at[4])
     fetch.start()
@@ -77,6 +81,7 @@
     buffers = {
         RIM: ((rim_x, got_rim_x), (rim_y, got_rim_y)),
         LOCAL: ((loc_x, got_loc_x), (loc_y, got_loc_y)),
+        BEHIND: ((row_x, got_row_x), (row_y, got_row_y)),
         SUMS: ((sum_x, got_sum_x), (sum_y, got_sum_y)),
     }
 
@@ -97,6 +102,10 @@
     def pair_slot(face, k):
         return tab[1, face * SHARED + k]
 
+    def grain_of(slot):
+        grain = grains[jnp.minimum(slot, slots - 1)]
+        return jnp.where(grain >= 0, grain, -1)
+
     def gather_columns(face, column, tiles):
         packed = zero
         for k in range(SHARED):
@@ -118,27 +127,26 @@
                     moved = pltpu.roll(packed, (edge - (k * depth + layer)) % cols, 1)
                     halo[at] = jnp.where(col == edge, moved, 0.0)
 
-    def totals(first):
+    def totals(first, keep=True):
         def body(slot, sums):
             held_pair = tab[0, slot]
             out_sums = []
             for layer in range(depth):
                 at = tile(slot, layer)
                 value = field[at] if first else local[at] + halo[tile(held_pair, layer)]
-                if not first:
+                if not first and keep:
                     field[at] = value
                 out_sums.append(sums[layer] + value * value)
             return tuple(out_sums)
 
-        return lax.fori_loop(0, slots, body, (zero,) * depth)
+        return lax.fori_loop(0, slots, body, (zero,) * depth, unroll=UNROLL)
 
     def update(sums):
         coefs = tuple(SELF - TOTAL * s for s in sums)
         below, above = planes[0], planes[1]
 
         def body(slot, carry):
-            grain = grains[slot]
-            grain = jnp.where(grain >= 0, grain, -1)
+            grain = grain_of(slot)
             values = [field[tile(slot, layer)] for layer in range(depth)]
             small = [LINK * v for v in values]
             low = jnp.where(below == grain, LINK, 0.0)
@@ -156,7 +164,7 @@
                 local[tile(slot, layer)] = v * (coefs[layer] + v * w) + near
             return carry
 
-        lax.fori_loop(0, slots, body, 0)
+        lax.fori_loop(0, slots, body, 0, unroll=UNROLL)
 
     loads[1].wait()
     sums = totals(True)
@@ -178,48 +186,58 @@
     update(sums)
 
     for face in range(2):
+        edge = 0 if face == 0 else rows - 1
+        for k in range(SHARED):
+            slot = pair_slot(face, k)
+            for layer in range(depth):
+                loc_x[face, layer, k : k + 1] = local[tile(slot, layer), edge : edge + 1]
+        copy(LOCAL, face).start()
+    for face in range(2, 4):
+        loc_y[face - 2] = gather_columns(face, 0 if face == 2 else cols - 1, local)
+        copy(LOCAL, face).start()
+
+    for face in range(2):
         edge, second = (0, 1) if face == 0 else (rows - 1, rows - 2)
         for k in range(SHARED):
             slot = pair_slot(face, k)
-            grain = grains[slot]
-            grain = jnp.where(grain >= 0, grain, -1)
-            for layer in range(depth):
-                at = tile(slot, layer)
-                loc_x[face, 0, layer, k : k + 1] = local[at, edge : edge + 1]
-                behind = local[at, second : second + 1]
+            grain = grain_of(slot)
+            for layer in range(depth):
+                behind = local[tile(slot, layer), second : second + 1]
                 if layer == 0:
                     behind = behind + jnp.where(planes[0, edge : edge + 1] == grain, 1.0, 0.0)
                 if layer == depth - 1:
                     behind = behind + jnp.where(planes[1, edge : edge + 1] == grain, 1.0, 0.0)
-                loc_x[face, 1, layer, k : k + 1] = behind
+                row_x[face, layer, k : k + 1] = behind
+        copy(BEHIND, face).start()
     for face in range(2, 4):
         edge, second = (0, 1) if face == 2 else (cols - 1, cols - 2)
-        loc_y[face - 2, 0] = gather_columns(face, edge, local)
         behind = gather_columns(face, second, local)
         for k in range(SHARED):
-            grain = grains[pair_slot(face, k)]
-            grain = jnp.where(grain >= 0, grain, -1)
+            grain = grain_of(pair_slot(face, k))
             for plane, layer in ((0, 0), (1, depth - 1)):
                 place = k * depth + layer
                 frozen = jnp.where(planes[plane] == grain, 1.0, 0.0)
                 moved = pltpu.roll(frozen, (place - edge) % cols, 1)
                 behind = behind + jnp.where(col == place, moved, 0.0)
-        loc_y[face - 2, 1] = behind
-    for face in range(FACES):
-        copy(LOCAL, face).start()
-
-    for face in range(FACES):
+        row_y[face - 2] = behind
+        copy(BEHIND, face).start()
+
+    for face in range(2, 4):
         wait_for(RIM, face)
-        if face < 2:
-            scatter(face, lambda layer, k: got_rim_x[face, layer, k : k + 1], None)
-        else:
-            scatter(face, None, LINK * got_rim_y[face - 2])
-    sums = totals(False)
-
+        scatter(face, None, LINK * got_rim_y[face - 2])
+    sums = totals(False, keep=False)
     for face in range(2):
         edge = 0 if face == 0 else rows - 1
         for layer in range(depth):
-            sum_x[face, layer : layer + 1] = sums[layer][edge : edge + 1]
+            across_it = loc_x[face, layer]
+            across_it = jnp.sum(across_it * across_it, axis=0, keepdims=True)
+            sum_x[face, layer : layer + 1] = sums[layer][edge : edge + 1] - across_it
+        copy(SUMS, face).start()
+
+    for face in range(2):
+        wait_for(RIM, face)
+        scatter(face, lambda layer, k: got_rim_x[face, layer, k : k + 1], None)
+    sums = totals(False)
     for face in range(2, 4):
         edge = 0 if face == 2 else cols - 1
         packed = zero
@@ -228,7 +246,6 @@
         two = packed + pltpu.roll(packed, depth, 1)
         four = two + pltpu.roll(two, 2 * depth, 1)
         sum_y[face - 2] = four + pltpu.roll(two, 4 * depth, 1)
-    for face in range(FACES):
         copy(SUMS, face).start()
 
     update(sums)
@@ -237,24 +254,25 @@
         wait_for(LOCAL, face)
         if face < 2:
             for layer in range(depth):
-                next_x[face, layer] = got_loc_x[face, 0, layer] + LINK * rim_x[face, layer]
+                next_x[face, layer] = got_loc_x[face, layer] + LINK * rim_x[face, layer]
             scatter(face, lambda layer, k: next_x[face, layer, k : k + 1], None)
         else:
-            next_y[face - 2] = got_loc_y[face - 2, 0] + LINK * rim_y[face - 2]
+            next_y[face - 2] = got_loc_y[face - 2] + LINK * rim_y[face - 2]
             scatter(face, None, LINK * next_y[face - 2])
     update(totals(False))
 
     group = lax.rem(col, depth)
     lane = col[:SHARED]
     for face in range(FACES):
+        wait_for(BEHIND, face)
         wait_for(SUMS, face)
         if face < 2:
             rims = [next_x[face, layer] for layer in range(depth)]
             for layer in range(depth):
                 r = rims[layer]
                 near = (
-                    got_loc_x[face, 1, layer]
-                    + loc_x[face, 0, layer]
+                    got_row_x[face, layer]
+                    + loc_x[face, layer]
                     + LINK * got_rim_x[face, layer]
                     + jnp.where(lane == cols - 1, 0.0, pltpu.roll(r, cols - 1, 1))
                     + jnp.where(lane == 0, 0.0, pltpu.roll(r, 1, 1))
@@ -263,14 +281,15 @@
                     near = near + rims[layer - 1]
                 if layer < depth - 1:
                     near = near + rims[layer + 1]
-                total = jnp.broadcast_to(got_sum_x[face, layer : layer + 1], r.shape)
+                total = got_sum_x[face, layer : layer + 1] + jnp.sum(r * r, axis=0, keepdims=True)
+                total = jnp.broadcast_to(total, r.shape)
                 next_x[face, layer] = r * (SELF - TOTAL * total + LINK * r * r) + LINK * near
             scatter(face, lambda layer, k: next_x[face, layer, k : k + 1], None)
         else:
             r = next_y[face - 2]
             near = (
-                got_loc_y[face - 2, 1]
-                + loc_y[face - 2, 0]
+                got_row_y[face - 2]
+                + loc_y[face - 2]
                 + LINK * got_rim_y[face - 2]
                 + jnp.where(row == rows - 1, 0.0, pltpu.roll(r, rows - 1, 0))
                 + jnp.where(row == 0, 0.0, pltpu.roll(r, 1, 0))
@@ -288,7 +307,7 @@
         return carry
 
     lax.fori_loop(0, slots, finish, 0)
-    for kind in (RIM, LOCAL, SUMS):
+    for kind in (RIM, LOCAL, BEHIND, SUMS):
         for face in range(FACES):
             copy(kind, face).wait_send()
 
@@ -300,10 +319,8 @@
         slots, depth, rows, cols = order_params.shape
         tiles = (slots * depth, rows, cols)
         rim_x = pltpu.VMEM((2, depth, SHARED, cols), jnp.float32)
-        loc_x = pltpu.VMEM((2, 2, depth, SHARED, cols), jnp.float32)
         sum_x = pltpu.VMEM((2, depth, cols), jnp.float32)
         rim_y = pltpu.VMEM((2, rows, cols), jnp.float32)
-        loc_y = pltpu.VMEM((2, 2, rows, cols), jnp.float32)
         operands = (channel_maps.reshape(FACES, slots), grain_ids.reshape(slots), zplanes, order_params.reshape(tiles))
         result = pl.pallas_call(
             functools.partial(kernel, slots, depth, nx, ny),
@@ -311,8 +328,8 @@
             in_specs=[pl.BlockSpec(memory_space=pltpu.HBM)] * 4,
             out_specs=pl.BlockSpec(memory_space=pltpu.VMEM),
             scratch_shapes=[
-                pltpu.VMEM(tiles, jnp.float32),
-                pltpu.VMEM(tiles, jnp.float32),
+                pltpu.VMEM(((slots + 1) * depth, rows, cols), jnp.float32),
+                pltpu.VMEM(((slots + 1) * depth, rows, cols), jnp.float32),
                 pltpu.VMEM(((FACES * SHARED + 1) * depth, rows, cols), jnp.float32),
                 pltpu.VMEM((FACES, slots), jnp.int32),
                 pltpu.VMEM((rows, cols), jnp.int32),
@@ -320,12 +337,12 @@
                 pltpu.SMEM((rows, cols), jnp.int32),
                 pltpu.SMEM((slots,), jnp.int32),
                 pltpu.VMEM((2, rows, cols), jnp.int32),
-                rim_x, rim_x, loc_x, loc_x, sum_x, sum_x,
-                rim_y, rim_y, loc_y, loc_y, rim_y, rim_y,
+                rim_x, rim_x, rim_x, rim_x, rim_x, rim_x, sum_x, sum_x,
+                rim_y, rim_y, rim_y, rim_y, rim_y, rim_y, rim_y, rim_y,
                 rim_x, rim_y,
                 pltpu.SemaphoreType.DMA((5,)),
-                pltpu.SemaphoreType.DMA((3, FACES)),
-                pltpu.SemaphoreType.DMA((3, FACES)),
+                pltpu.SemaphoreType.DMA((4, FACES)),
+                pltpu.SemaphoreType.DMA((4, FACES)),
             ],
             compiler_params=pltpu.CompilerParams(
                 collective_id=0, has_side_effects=True, vmem_limit_bytes=16 * 2**20

time: 20.9 us -> 18.6 us (0.89)
  Pallas kernels: 19.8 us -> 17.4 us
    pallas_call x1, Pallas kernels: 19.8 us -> 17.4 us  [on_device(): pl.pallas_call(functools.partial(kernel, slots, depth, nx, ny), out_shape...]
where the time goes in v3:
time: 18.6 us; the launch traced here: 18.5 us
  Pallas kernels  17.4 us (94%)
  local copies, waits for them, and re-layouts  1.02 us (5%)
    pallas_call x1, Pallas kernels, on_device(): pl.pallas_call(functools.partial(kernel, slots, depth, nx, ny), out_shape...  17.4 us
    unnamed x1, local copies, waits for them, and re-layouts  1.02 us

profile of v3, /device:TPU:1, one launch (start us, length us, event | category | flops | bytes accessed | tf_op | source)
XLA Modules:
  0.0 18.5 jit_solution(704911833475892313)
XLA Ops:
  0.0 17.4 %shard_map.46 = f32[288,8,128]{2,1,0:T(8,128)S(1)} custom-call(s32[4,24]{1,0:T(4,128)} %bitcast.6, s32[24]{0:T(128)} %bitcast.7, s32[2,8,128]{2,1,0:T(8,128)} %planes_in.1, f32[288,8,128]{2,1,0:T(8,128)} %bitcast.5), custom_call_target="tpu_custom_call" | custom-call | tf_op jit(solution)/shard_map/pallas_call | solution.py:325
  17.5 1.0 %copy.6 = f32[24,12,8,128]{3,2,1,0:T(8,128)} copy(f32[24,12,8,128]{3,2,1,0:T(8,128)S(1)} %bitcast.4) | data formatting | bytes 2359296

commit v4 on v3

--- a/solution.py
+++ b/solution.py
@@ -15,13 +15,13 @@
 TOTAL = 0.15
 LINK = 0.1
 
-RIM, LOCAL, BEHIND, SUMS = 0, 1, 2, 3
+RIM, LOCAL, BEHIND, SUMS, CORNER = 0, 1, 2, 3, 4
 UNROLL = 8
 
 
-def kernel(slots, depth, nx, ny, maps_in, grains_in, planes_in, start, out, field, local, halo, maps, key_box, table, tab,
+def kernel(slots, depth, nx, ny, maps_in, grains_in, planes_in, start, out, field, local, halo, halo2, maps, key_box, table, tab,
            grains, planes, rim_x, got_rim_x, loc_x, got_loc_x, row_x, got_row_x, sum_x, got_sum_x, rim_y, got_rim_y, loc_y,
-           got_loc_y, row_y, got_row_y, sum_y, got_sum_y, next_x, next_y, load_sem, send_sem, recv_sem):
+           got_loc_y, row_y, got_row_y, sum_y, got_sum_y, next_x, next_y, cor_y, got_cor_y, got_cor_x, load_sem, send_sem, recv_sem):
     rows, cols = 8, 128
     i, j = lax.axis_index("gx"), lax.axis_index("gy")
     across = (
@@ -44,6 +44,7 @@
 
     row = lax.broadcasted_iota(jnp.int32, (rows, cols), 0)
     col = lax.broadcasted_iota(jnp.int32, (rows, cols), 1)
+    lane = col[:SHARED]
     zero = jnp.zeros((rows, cols), jnp.float32)
 
     def tile(slot, layer):
@@ -52,6 +53,7 @@
     def clear(slot, carry):
         for layer in range(depth):
             halo[tile(slot, layer)] = zero
+            halo2[tile(slot, layer)] = zero
         return carry
 
     lax.fori_loop(0, slots + 1, clear, 0)
@@ -83,13 +85,18 @@
         LOCAL: ((loc_x, got_loc_x), (loc_y, got_loc_y)),
         BEHIND: ((row_x, got_row_x), (row_y, got_row_y)),
         SUMS: ((sum_x, got_sum_x), (sum_y, got_sum_y)),
+        CORNER: (None, (cor_y, got_cor_y)),
     }
 
     def copy(kind, face):
-        sent, got = buffers[kind][face // 2]
+        if kind == CORNER and face < 2:
+            source, target = got_cor_y.at[:, face], got_cor_x.at[1 - face]
+        else:
+            sent, got = buffers[kind][face // 2]
+            source, target = sent.at[face % 2], got.at[1 - face % 2]
         return pltpu.make_async_remote_copy(
-            src_ref=sent.at[face % 2],
-            dst_ref=got.at[1 - face % 2],
+            src_ref=source,
+            dst_ref=target,
             send_sem=send_sem.at[kind, face],
             recv_sem=recv_sem.at[kind, face ^ 1],
             device_id=across[face],
@@ -116,7 +123,18 @@
                 packed = jnp.where(col == place, moved, packed)
         return packed
 
-    def scatter(face, layer_row, packed):
+    def corners(rims, column):
+        packed = jnp.zeros((SHARED, cols), jnp.float32)
+        for layer in range(depth):
+            packed = jnp.where(lane == layer, pltpu.roll(rims[layer], (layer - column) % cols, 1), packed)
+        return packed
+
+    def per_pair(layers):
+        two = layers + pltpu.roll(layers, depth, 1)
+        four = two + pltpu.roll(two, 2 * depth, 1)
+        return four + pltpu.roll(two, 4 * depth, 1)
+
+    def scatter(face, layer_row, packed, halo=halo):
         edge = 0 if face % 2 == 0 else (rows if face < 2 else cols) - 1
         for k in range(SHARED):
             for layer in range(depth):
@@ -127,7 +145,7 @@
                     moved = pltpu.roll(packed, (edge - (k * depth + layer)) % cols, 1)
                     halo[at] = jnp.where(col == edge, moved, 0.0)
 
-    def totals(first, keep=True):
+    def totals(first, halo=halo, keep=True):
         def body(slot, sums):
             held_pair = tab[0, slot]
             out_sums = []
@@ -180,6 +198,11 @@
     pl.semaphore_wait(barrier, FACES)
     for face in range(FACES):
         copy(RIM, face).start()
+    for face in range(2, 4):
+        for other in range(2):
+            rims = [rim_x[other, layer] for layer in range(depth)]
+            cor_y[face - 2, other] = corners(rims, 0 if face == 2 else cols - 1)
+        copy(CORNER, face).start()
 
     loads[2].wait()
     loads[3].wait()
@@ -219,9 +242,16 @@
                 frozen = jnp.where(planes[plane] == grain, 1.0, 0.0)
                 moved = pltpu.roll(frozen, (place - edge) % cols, 1)
                 behind = behind + jnp.where(col == place, moved, 0.0)
-        row_y[face - 2] = behind
+        row_y[face - 2, 0] = behind
+        for other in range(2):
+            rims = [loc_x[other, layer] for layer in range(depth)]
+            row_y[face - 2, 1 + other, 0:SHARED] = corners(rims, edge)
         copy(BEHIND, face).start()
 
+    for face in range(2, 4):
+        wait_for(CORNER, face)
+    for face in range(2):
+        copy(CORNER, face).start()
     for face in range(2, 4):
         wait_for(RIM, face)
         scatter(face, None, LINK * got_rim_y[face - 2])
@@ -233,36 +263,34 @@
             across_it = jnp.sum(across_it * across_it, axis=0, keepdims=True)
             sum_x[face, layer : layer + 1] = sums[layer][edge : edge + 1] - across_it
         copy(SUMS, face).start()
+    for face in range(2, 4):
+        edge = 0 if face == 2 else cols - 1
+        packed = zero
+        for layer in range(depth):
+            packed = jnp.where(col == layer, pltpu.roll(sums[layer], (layer - edge) % cols, 1), packed)
+        sum_y[face - 2] = per_pair(packed)
+        copy(SUMS, face).start()
+
+    for face in range(2, 4):
+        wait_for(LOCAL, face)
+        next_y[face - 2] = got_loc_y[face - 2] + LINK * rim_y[face - 2]
+        scatter(face, None, LINK * next_y[face - 2], halo2)
 
     for face in range(2):
         wait_for(RIM, face)
         scatter(face, lambda layer, k: got_rim_x[face, layer, k : k + 1], None)
-    sums = totals(False)
-    for face in range(2, 4):
-        edge = 0 if face == 2 else cols - 1
-        packed = zero
-        for layer in range(depth):
-            packed = jnp.where(col == layer, pltpu.roll(sums[layer], (layer - edge) % cols, 1), packed)
-        two = packed + pltpu.roll(packed, depth, 1)
-        four = two + pltpu.roll(two, 2 * depth, 1)
-        sum_y[face - 2] = four + pltpu.roll(two, 4 * depth, 1)
-        copy(SUMS, face).start()
-
-    update(sums)
-
-    for face in range(FACES):
+    update(totals(False))
+
+    for face in range(2):
         wait_for(LOCAL, face)
-        if face < 2:
-            for layer in range(depth):
-                next_x[face, layer] = got_loc_x[face, layer] + LINK * rim_x[face, layer]
-            scatter(face, lambda layer, k: next_x[face, layer, k : k + 1], None)
-        else:
-            next_y[face - 2] = got_loc_y[face - 2] + LINK * rim_y[face - 2]
-            scatter(face, None, LINK * next_y[face - 2])
-    update(totals(False))
+        for layer in range(depth):
+            next_x[face, layer] = got_loc_x[face, layer] + LINK * rim_x[face, layer]
+        scatter(face, lambda layer, k: next_x[face, layer, k : k + 1], None, halo2)
+    update(totals(False, halo2))
 
     group = lax.rem(col, depth)
-    lane = col[:SHARED]
+    for face in range(2):
+        wait_for(CORNER, face)
     for face in range(FACES):
         wait_for(BEHIND, face)
         wait_for(SUMS, face)
@@ -288,7 +316,7 @@
         else:
             r = next_y[face - 2]
             near = (
-                got_row_y[face - 2]
+                got_row_y[face - 2, 0]
                 + loc_y[face - 2]
                 + LINK * got_rim_y[face - 2]
                 + jnp.where(row == rows - 1, 0.0, pltpu.roll(r, rows - 1, 0))
@@ -297,6 +325,11 @@
                 + jnp.where(group == 0, 0.0, pltpu.roll(r, 1, 1))
             )
             total = got_sum_y[face - 2]
+            for other in range(2):
+                h, g = got_cor_x[other, face - 2], got_row_y[face - 2, 1 + other, 0:SHARED]
+                more = jnp.sum(LINK * h * (2.0 * g + LINK * h), axis=0, keepdims=True)
+                more = per_pair(jnp.broadcast_to(more, (rows, cols)))
+                total = total + jnp.where(row == (0 if other == 0 else rows - 1), more, 0.0)
             scatter(face, None, LINK * (r * (SELF - TOTAL * total + LINK * r * r) + LINK * near))
 
     def finish(slot, carry):
@@ -307,7 +340,7 @@
         return carry
 
     lax.fori_loop(0, slots, finish, 0)
-    for kind in (RIM, LOCAL, BEHIND, SUMS):
+    for kind in (RIM, LOCAL, BEHIND, SUMS, CORNER):
         for face in range(FACES):
             copy(kind, face).wait_send()
 
@@ -321,6 +354,8 @@
         rim_x = pltpu.VMEM((2, depth, SHARED, cols), jnp.float32)
         sum_x = pltpu.VMEM((2, depth, cols), jnp.float32)
         rim_y = pltpu.VMEM((2, rows, cols), jnp.float32)
+        row_y = pltpu.VMEM((2, 3, rows, cols), jnp.float32)
+        corner = pltpu.VMEM((2, 2, SHARED, cols), jnp.float32)
         operands = (channel_maps.reshape(FACES, slots), grain_ids.reshape(slots), zplanes, order_params.reshape(tiles))
         result = pl.pallas_call(
             functools.partial(kernel, slots, depth, nx, ny),
@@ -331,6 +366,7 @@
                 pltpu.VMEM(((slots + 1) * depth, rows, cols), jnp.float32),
                 pltpu.VMEM(((slots + 1) * depth, rows, cols), jnp.float32),
                 pltpu.VMEM(((FACES * SHARED + 1) * depth, rows, cols), jnp.float32),
+                pltpu.VMEM(((FACES * SHARED + 1) * depth, rows, cols), jnp.float32),
                 pltpu.VMEM((FACES, slots), jnp.int32),
                 pltpu.VMEM((rows, cols), jnp.int32),
                 pltpu.VMEM((rows, cols), jnp.int32),
@@ -338,11 +374,11 @@
                 pltpu.SMEM((slots,), jnp.int32),
                 pltpu.VMEM((2, rows, cols), jnp.int32),
                 rim_x, rim_x, rim_x, rim_x, rim_x, rim_x, sum_x, sum_x,
-                rim_y, rim_y, rim_y, rim_y, rim_y, rim_y, rim_y, rim_y,
-                rim_x, rim_y,
+                rim_y, rim_y, rim_y, rim_y, row_y, row_y, rim_y, rim_y,
+                rim_x, rim_y, corner, corner, corner,
                 pltpu.SemaphoreType.DMA((5,)),
-                pltpu.SemaphoreType.DMA((4, FACES)),
-                pltpu.SemaphoreType.DMA((4, FACES)),
+                pltpu.SemaphoreType.DMA((5, FACES)),
+                pltpu.SemaphoreType.DMA((5, FACES)),
             ],
             compiler_params=pltpu.CompilerParams(
                 collective_id=0, has_side_effects=True, vmem_limit_bytes=16 * 2**20

time: 18.6 us -> 18.6 us (level)
  no operation moved by 1% of the time
where the time goes in v4:
time: 18.6 us; the launch traced here: 18.5 us
  Pallas kernels  17.5 us (94%)
  local copies, waits for them, and re-layouts  1.02 us (5%)
    pallas_call x1, Pallas kernels, on_device(): pl.pallas_call(functools.partial(kernel, slots, depth, nx, ny), out_shape...  17.5 us
    unnamed x1, local copies, waits for them, and re-layouts  1.02 us

profile of v4, /device:TPU:1, one launch (start us, length us, event | category | flops | bytes accessed | tf_op | source)
XLA Modules:
  0.0 18.5 jit_solution(7532819888222856402)
XLA Ops:
  0.0 17.5 %shard_map.46 = f32[288,8,128]{2,1,0:T(8,128)S(1)} custom-call(s32[4,24]{1,0:T(4,128)} %bitcast.6, s32[24]{0:T(128)} %bitcast.7, s32[2,8,128]{2,1,0:T(8,128)} %planes_in.1, f32[288,8,128]{2,1,0:T(8,128)} %bitcast.5), custom_call_target="tpu_custom_call" | custom-call | tf_op jit(solution)/shard_map/pallas_call | solution.py:360
  17.5 1.0 %copy.6 = f32[24,12,8,128]{3,2,1,0:T(8,128)} copy(f32[24,12,8,128]{3,2,1,0:T(8,128)S(1)} %bitcast.4) | data formatting | bytes 2359296

commit v5 on v4

--- a/solution.py
+++ b/solution.py
@@ -21,7 +21,7 @@
 
 def kernel(slots, depth, nx, ny, maps_in, grains_in, planes_in, start, out, field, local, halo, halo2, maps, key_box, table, tab,
            grains, planes, rim_x, got_rim_x, loc_x, got_loc_x, row_x, got_row_x, sum_x, got_sum_x, rim_y, got_rim_y, loc_y,
-           got_loc_y, row_y, got_row_y, sum_y, got_sum_y, next_x, next_y, cor_y, got_cor_y, got_cor_x, load_sem, send_sem, recv_sem):
+           got_loc_y, row_y, got_row_y, sum_y, got_sum_y, next_x, next_y, ice_x, cor_y, got_cor_y, got_cor_x, load_sem, send_sem, recv_sem):
     rows, cols = 8, 128
     i, j = lax.axis_index("gx"), lax.axis_index("gy")
     across = (
@@ -45,6 +45,7 @@
     row = lax.broadcasted_iota(jnp.int32, (rows, cols), 0)
     col = lax.broadcasted_iota(jnp.int32, (rows, cols), 1)
     lane = col[:SHARED]
+    group = lax.rem(col, depth)
     zero = jnp.zeros((rows, cols), jnp.float32)
 
     def tile(slot, layer):
@@ -111,7 +112,7 @@
 
     def grain_of(slot):
         grain = grains[jnp.minimum(slot, slots - 1)]
-        return jnp.where(grain >= 0, grain, -1)
+        return jnp.where((grain >= 0) & (slot < slots), grain, -1)
 
     def gather_columns(face, column, tiles):
         packed = zero
@@ -133,6 +134,34 @@
         two = layers + pltpu.roll(layers, depth, 1)
         four = two + pltpu.roll(two, 2 * depth, 1)
         return four + pltpu.roll(two, 4 * depth, 1)
+
+    def columns_of(layers, column):
+        packed = zero
+        for layer in range(depth):
+            packed = jnp.where(col == layer, pltpu.roll(layers[layer], (layer - column) % cols, 1), packed)
+        return packed
+
+    def step_x(r, layer, rims, total, beside):
+        near = (
+            beside
+            + jnp.where(lane == cols - 1, 0.0, pltpu.roll(r, cols - 1, 1))
+            + jnp.where(lane == 0, 0.0, pltpu.roll(r, 1, 1))
+        )
+        if layer:
+            near = near + rims[layer - 1]
+        if layer < depth - 1:
+            near = near + rims[layer + 1]
+        return r * (SELF - TOTAL * total + LINK * r * r) + LINK * near
+
+    def step_y(r, total, beside):
+        near = (
+            beside
+            + jnp.where(row == rows - 1, 0.0, pltpu.roll(r, rows - 1, 0))
+            + jnp.where(row == 0, 0.0, pltpu.roll(r, 1, 0))
+            + jnp.where(group == depth - 1, 0.0, pltpu.roll(r, cols - 1, 1))
+            + jnp.where(group == 0, 0.0, pltpu.roll(r, 1, 1))
+        )
+        return r * (SELF - TOTAL * total + LINK * r * r) + LINK * near
 
     def scatter(face, layer_row, packed, halo=halo):
         edge = 0 if face % 2 == 0 else (rows if face < 2 else cols) - 1
@@ -182,7 +211,7 @@
                 local[tile(slot, layer)] = v * (coefs[layer] + v * w) + near
             return carry
 
-        lax.fori_loop(0, slots, body, 0, unroll=UNROLL)
+        lax.fori_loop(0, slots, body, 0, unroll=slots)
 
     loads[1].wait()
     sums = totals(True)
@@ -198,51 +227,65 @@
     pl.semaphore_wait(barrier, FACES)
     for face in range(FACES):
         copy(RIM, face).start()
+
+    loads[2].wait()
+    loads[3].wait()
+    for face in range(2):
+        edge, second = (0, 1) if face == 0 else (rows - 1, rows - 2)
+        for k in range(SHARED):
+            slot = pair_slot(face, k)
+            grain = grain_of(slot)
+            for plane in range(2):
+                ice_x[face, plane, k : k + 1] = jnp.where(planes[plane, edge : edge + 1] == grain, 1.0, 0.0)
+            for layer in range(depth):
+                row_x[face, layer, k : k + 1] = field[tile(slot, layer), second : second + 1]
+        rims = [rim_x[face, layer] for layer in range(depth)]
+        for layer in range(depth):
+            beside = row_x[face, layer]
+            if layer == 0:
+                beside = beside + ice_x[face, 0]
+            if layer == depth - 1:
+                beside = beside + ice_x[face, 1]
+            total = jnp.broadcast_to(sums[layer][edge : edge + 1], beside.shape)
+            loc_x[face, layer] = step_x(rims[layer], layer, rims, total, beside)
+        copy(LOCAL, face).start()
+    ice_y = []
+    for face in range(2, 4):
+        edge, second = (0, 1) if face == 2 else (cols - 1, cols - 2)
+        ice = zero
+        for k in range(SHARED):
+            grain = grain_of(pair_slot(face, k))
+            for plane, layer in ((0, 0), (1, depth - 1)):
+                place = k * depth + layer
+                frozen = jnp.where(planes[plane] == grain, 1.0, 0.0)
+                ice = jnp.where(col == place, pltpu.roll(frozen, (place - edge) % cols, 1), ice)
+        ice_y.append(ice)
+        total = per_pair(columns_of(sums, edge))
+        loc_y[face - 2] = step_y(rim_y[face - 2], total, gather_columns(face, second, field) + ice)
+        copy(LOCAL, face).start()
     for face in range(2, 4):
         for other in range(2):
             rims = [rim_x[other, layer] for layer in range(depth)]
             cor_y[face - 2, other] = corners(rims, 0 if face == 2 else cols - 1)
         copy(CORNER, face).start()
 
-    loads[2].wait()
-    loads[3].wait()
     update(sums)
 
     for face in range(2):
-        edge = 0 if face == 0 else rows - 1
+        second = 1 if face == 0 else rows - 2
         for k in range(SHARED):
             slot = pair_slot(face, k)
-            for layer in range(depth):
-                loc_x[face, layer, k : k + 1] = local[tile(slot, layer), edge : edge + 1]
-        copy(LOCAL, face).start()
-    for face in range(2, 4):
-        loc_y[face - 2] = gather_columns(face, 0 if face == 2 else cols - 1, local)
-        copy(LOCAL, face).start()
-
-    for face in range(2):
-        edge, second = (0, 1) if face == 0 else (rows - 1, rows - 2)
-        for k in range(SHARED):
-            slot = pair_slot(face, k)
-            grain = grain_of(slot)
             for layer in range(depth):
                 behind = local[tile(slot, layer), second : second + 1]
                 if layer == 0:
-                    behind = behind + jnp.where(planes[0, edge : edge + 1] == grain, 1.0, 0.0)
+                    behind = behind + ice_x[face, 0, k : k + 1]
                 if layer == depth - 1:
-                    behind = behind + jnp.where(planes[1, edge : edge + 1] == grain, 1.0, 0.0)
+                    behind = behind + ice_x[face, 1, k : k + 1]
                 row_x[face, layer, k : k + 1] = behind
         copy(BEHIND, face).start()
     for face in range(2, 4):
         edge, second = (0, 1) if face == 2 else (cols - 1, cols - 2)
-        behind = gather_columns(face, second, local)
-        for k in range(SHARED):
-            grain = grain_of(pair_slot(face, k))
-            for plane, layer in ((0, 0), (1, depth - 1)):
-                place = k * depth + layer
-                frozen = jnp.where(planes[plane] == grain, 1.0, 0.0)
-                moved = pltpu.roll(frozen, (place - edge) % cols, 1)
-                behind = behind + jnp.where(col == place, moved, 0.0)
-        row_y[face - 2, 0] = behind
+        row_y[face - 2, 0] = gather_columns(face, second, local) + ice_y[face - 2]
         for other in range(2):
             rims = [loc_x[other, layer] for layer in range(depth)]
             row_y[face - 2, 1 + other, 0:SHARED] = corners(rims, edge)
@@ -265,10 +308,7 @@
         copy(SUMS, face).start()
     for face in range(2, 4):
         edge = 0 if face == 2 else cols - 1
-        packed = zero
-        for layer in range(depth):
-            packed = jnp.where(col == layer, pltpu.roll(sums[layer], (layer - edge) % cols, 1), packed)
-        sum_y[face - 2] = per_pair(packed)
+        sum_y[face - 2] = per_pair(columns_of(sums, edge))
         copy(SUMS, face).start()
 
     for face in range(2, 4):
@@ -288,7 +328,6 @@
         scatter(face, lambda layer, k: next_x[face, layer, k : k + 1], None, halo2)
     update(totals(False, halo2))
 
-    group = lax.rem(col, depth)
     for face in range(2):
         wait_for(CORNER, face)
     for face in range(FACES):
@@ -298,39 +337,19 @@
             rims = [next_x[face, layer] for layer in range(depth)]
             for layer in range(depth):
                 r = rims[layer]
-                near = (
-                    got_row_x[face, layer]
-                    + loc_x[face, layer]
-                    + LINK * got_rim_x[face, layer]
-                    + jnp.where(lane == cols - 1, 0.0, pltpu.roll(r, cols - 1, 1))
-                    + jnp.where(lane == 0, 0.0, pltpu.roll(r, 1, 1))
-                )
-                if layer:
-                    near = near + rims[layer - 1]
-                if layer < depth - 1:
-                    near = near + rims[layer + 1]
+                beside = got_row_x[face, layer] + loc_x[face, layer] + LINK * got_rim_x[face, layer]
                 total = got_sum_x[face, layer : layer + 1] + jnp.sum(r * r, axis=0, keepdims=True)
-                total = jnp.broadcast_to(total, r.shape)
-                next_x[face, layer] = r * (SELF - TOTAL * total + LINK * r * r) + LINK * near
+                next_x[face, layer] = step_x(r, layer, rims, jnp.broadcast_to(total, r.shape), beside)
             scatter(face, lambda layer, k: next_x[face, layer, k : k + 1], None)
         else:
-            r = next_y[face - 2]
-            near = (
-                got_row_y[face - 2, 0]
-                + loc_y[face - 2]
-                + LINK * got_rim_y[face - 2]
-                + jnp.where(row == rows - 1, 0.0, pltpu.roll(r, rows - 1, 0))
-                + jnp.where(row == 0, 0.0, pltpu.roll(r, 1, 0))
-                + jnp.where(group == depth - 1, 0.0, pltpu.roll(r, cols - 1, 1))
-                + jnp.where(group == 0, 0.0, pltpu.roll(r, 1, 1))
-            )
+            beside = got_row_y[face - 2, 0] + loc_y[face - 2] + LINK * got_rim_y[face - 2]
             total = got_sum_y[face - 2]
             for other in range(2):
                 h, g = got_cor_x[other, face - 2], got_row_y[face - 2, 1 + other, 0:SHARED]
                 more = jnp.sum(LINK * h * (2.0 * g + LINK * h), axis=0, keepdims=True)
                 more = per_pair(jnp.broadcast_to(more, (rows, cols)))
                 total = total + jnp.where(row == (0 if other == 0 else rows - 1), more, 0.0)
-            scatter(face, None, LINK * (r * (SELF - TOTAL * total + LINK * r * r) + LINK * near))
+            scatter(face, None, LINK * step_y(next_y[face - 2], total, beside))
 
     def finish(slot, carry):
         held_pair = tab[0, slot]
@@ -355,6 +374,7 @@
         sum_x = pltpu.VMEM((2, depth, cols), jnp.float32)
         rim_y = pltpu.VMEM((2, rows, cols), jnp.float32)
         row_y = pltpu.VMEM((2, 3, rows, cols), jnp.float32)
+        ice_x = pltpu.VMEM((2, 2, SHARED, cols), jnp.float32)
         corner = pltpu.VMEM((2, 2, SHARED, cols), jnp.float32)
         operands = (channel_maps.reshape(FACES, slots), grain_ids.reshape(slots), zplanes, order_params.reshape(tiles))
         result = pl.pallas_call(
@@ -375,7 +395,7 @@
                 pltpu.VMEM((2, rows, cols), jnp.int32),
                 rim_x, rim_x, rim_x, rim_x, rim_x, rim_x, sum_x, sum_x,
                 rim_y, rim_y, rim_y, rim_y, row_y, row_y, rim_y, rim_y,
-                rim_x, rim_y, corner, corner, corner,
+                rim_x, rim_y, ice_x, corner, corner, corner,
                 pltpu.SemaphoreType.DMA((5,)),
                 pltpu.SemaphoreType.DMA((5, FACES)),
                 pltpu.SemaphoreType.DMA((5, FACES)),

time: 18.6 us -> 18.7 us (level)
  no operation moved by 1% of the time
where the time goes in v5:
time: 18.7 us; the launch traced here: 18.6 us
  Pallas kernels  17.6 us (94%)
  local copies, waits for them, and re-layouts  1.02 us (5%)
    pallas_call x1, Pallas kernels, on_device(): pl.pallas_call(functools.partial(kernel, slots, depth, nx, ny), out_shape...  17.6 us
    unnamed x1, local copies, waits for them, and re-layouts  1.02 us

profile of v5, /device:TPU:1, one launch (start us, length us, event | category | flops | bytes accessed | tf_op | source)
XLA Modules:
  0.0 18.6 jit_solution(9178725541090212756)
XLA Ops:
  0.0 17.6 %shard_map.46 = f32[288,8,128]{2,1,0:T(8,128)S(1)} custom-call(s32[4,24]{1,0:T(4,128)} %bitcast.6, s32[24]{0:T(128)} %bitcast.7, s32[2,8,128]{2,1,0:T(8,128)} %planes_in.1, f32[288,8,128]{2,1,0:T(8,128)} %bitcast.5), custom_call_target="tpu_custom_call" | custom-call | tf_op jit(solution)/shard_map/pallas_call | solution.py:380
  17.6 1.0 %copy.6 = f32[24,12,8,128]{3,2,1,0:T(8,128)} copy(f32[24,12,8,128]{3,2,1,0:T(8,128)S(1)} %bitcast.4) | data formatting | bytes 2359296

commit v6 on v5

--- a/solution.py
+++ b/solution.py
@@ -46,6 +46,7 @@
     col = lax.broadcasted_iota(jnp.int32, (rows, cols), 1)
     lane = col[:SHARED]
     group = lax.rem(col, depth)
+    deep_row, deep_col = (lax.broadcasted_iota(jnp.int32, (depth, cols), d) for d in range(2))
     zero = jnp.zeros((rows, cols), jnp.float32)
 
     def tile(slot, layer):
@@ -163,6 +164,11 @@
         )
         return r * (SELF - TOTAL * total + LINK * r * r) + LINK * near
 
+    def over_pairs(packed):
+        half = packed + pltpu.roll(packed, cols - 3 * depth, 1)
+        whole = half + pltpu.roll(half, cols - depth, 1) + pltpu.roll(half, cols - 2 * depth, 1)
+        return jnp.where(col < depth, whole, 0.0)
+
     def scatter(face, layer_row, packed, halo=halo):
         edge = 0 if face % 2 == 0 else (rows if face < 2 else cols) - 1
         for k in range(SHARED):
@@ -174,15 +180,24 @@
                     moved = pltpu.roll(packed, (edge - (k * depth + layer)) % cols, 1)
                     halo[at] = jnp.where(col == edge, moved, 0.0)
 
-    def totals(first, halo=halo, keep=True):
+    def totals_of(tiles):
+        def body(slot, sums):
+            out_sums = []
+            for layer in range(depth):
+                value = tiles[tile(slot, layer)]
+                out_sums.append(sums[layer] + value * value)
+            return tuple(out_sums)
+
+        return lax.fori_loop(0, slots, body, (zero,) * depth, unroll=UNROLL)
+
+    def totals(halo):
         def body(slot, sums):
             held_pair = tab[0, slot]
             out_sums = []
             for layer in range(depth):
                 at = tile(slot, layer)
-                value = field[at] if first else local[at] + halo[tile(held_pair, layer)]
-                if not first and keep:
-                    field[at] = value
+                value = local[at] + halo[tile(held_pair, layer)]
+                field[at] = value
                 out_sums.append(sums[layer] + value * value)
             return tuple(out_sums)
 
@@ -214,7 +229,7 @@
         lax.fori_loop(0, slots, body, 0, unroll=slots)
 
     loads[1].wait()
-    sums = totals(True)
+    sums = totals_of(field)
     fetch.wait()
     for face in range(2):
         edge = 0 if face == 0 else rows - 1
@@ -227,6 +242,11 @@
     pl.semaphore_wait(barrier, FACES)
     for face in range(FACES):
         copy(RIM, face).start()
+    for face in range(2, 4):
+        for other in range(2):
+            rims = [rim_x[other, layer] for layer in range(depth)]
+            cor_y[face - 2, other] = corners(rims, 0 if face == 2 else cols - 1)
+        copy(CORNER, face).start()
 
     loads[2].wait()
     loads[3].wait()
@@ -263,11 +283,6 @@
         total = per_pair(columns_of(sums, edge))
         loc_y[face - 2] = step_y(rim_y[face - 2], total, gather_columns(face, second, field) + ice)
         copy(LOCAL, face).start()
-    for face in range(2, 4):
-        for other in range(2):
-            rims = [rim_x[other, layer] for layer in range(depth)]
-            cor_y[face - 2, other] = corners(rims, 0 if face == 2 else cols - 1)
-        copy(CORNER, face).start()
 
     update(sums)
 
@@ -291,25 +306,37 @@
             row_y[face - 2, 1 + other, 0:SHARED] = corners(rims, edge)
         copy(BEHIND, face).start()
 
-    for face in range(2, 4):
-        wait_for(CORNER, face)
-    for face in range(2):
-        copy(CORNER, face).start()
-    for face in range(2, 4):
-        wait_for(RIM, face)
-        scatter(face, None, LINK * got_rim_y[face - 2])
-    sums = totals(False, keep=False)
+    sums = totals_of(local)
+    for face in range(2, 4):
+        edge = 0 if face == 2 else cols - 1
+        rims = loc_y[face - 2]
+        sum_y[face - 2] = per_pair(columns_of(sums, edge) - over_pairs(rims * rims))
+        copy(SUMS, face).start()
     for face in range(2):
         edge = 0 if face == 0 else rows - 1
         for layer in range(depth):
             across_it = loc_x[face, layer]
             across_it = jnp.sum(across_it * across_it, axis=0, keepdims=True)
             sum_x[face, layer : layer + 1] = sums[layer][edge : edge + 1] - across_it
+    for face in range(2, 4):
+        wait_for(RIM, face)
+        edge = 0 if face == 2 else cols - 1
+        h = got_rim_y[face - 2]
+        more = over_pairs(LINK * h * (2.0 * loc_y[face - 2] + LINK * h))
+        for other in range(2):
+            line = more[0:1] if other == 0 else more[rows - 1 : rows]
+            line = jnp.where(deep_col == deep_row, jnp.broadcast_to(line, (depth, cols)), 0.0)
+            line = jnp.sum(line, axis=1, keepdims=True)
+            sum_x[other] = sum_x[other] + jnp.where(deep_col == edge, jnp.broadcast_to(line, (depth, cols)), 0.0)
+    for face in range(2):
         copy(SUMS, face).start()
     for face in range(2, 4):
-        edge = 0 if face == 2 else cols - 1
-        sum_y[face - 2] = per_pair(columns_of(sums, edge))
-        copy(SUMS, face).start()
+        wait_for(CORNER, face)
+    for face in range(2):
+        copy(CORNER, face).start()
+
+    for face in range(2, 4):
+        scatter(face, None, LINK * got_rim_y[face - 2])
 
     for face in range(2, 4):
         wait_for(LOCAL, face)
@@ -319,14 +346,14 @@
     for face in range(2):
         wait_for(RIM, face)
         scatter(face, lambda layer, k: got_rim_x[face, layer, k : k + 1], None)
-    update(totals(False))
+    update(totals(halo))
 
     for face in range(2):
         wait_for(LOCAL, face)
         for layer in range(depth):
             next_x[face, layer] = got_loc_x[face, layer] + LINK * rim_x[face, layer]
         scatter(face, lambda layer, k: next_x[face, layer, k : k + 1], None, halo2)
-    update(totals(False, halo2))
+    update(totals(halo2))
 
     for face in range(2):
         wait_for(CORNER, face)
@@ -343,7 +370,8 @@
             scatter(face, lambda layer, k: next_x[face, layer, k : k + 1], None)
         else:
             beside = got_row_y[face - 2, 0] + loc_y[face - 2] + LINK * got_rim_y[face - 2]
-            total = got_sum_y[face - 2]
+            rims = next_y[face - 2]
+            total = got_sum_y[face - 2] + per_pair(over_pairs(rims * rims))
             for other in range(2):
                 h, g = got_cor_x[other, face - 2], got_row_y[face - 2, 1 + other, 0:SHARED]
                 more = jnp.sum(LINK * h * (2.0 * g + LINK * h), axis=0, keepdims=True)

time: 18.7 us -> 18 us (0.963)
  Pallas kernels: 17.6 us -> 16.9 us
    pallas_call x1, Pallas kernels: 17.6 us -> 16.9 us  [on_device(): pl.pallas_call(functools.partial(kernel, slots, depth, nx, ny), out_shape...]
where the time goes in v6:
time: 18 us; the launch traced here: 17.9 us
  Pallas kernels  16.9 us (94%)
  local copies, waits for them, and re-layouts  1.02 us (6%)
    pallas_call x1, Pallas kernels, on_device(): pl.pallas_call(functools.partial(kernel, slots, depth, nx, ny), out_shape...  16.9 us
    unnamed x1, local copies, waits for them, and re-layouts  1.02 us

profile of v6, /device:TPU:1, one launch (start us, length us, event | category | flops | bytes accessed | tf_op | source)
XLA Modules:
  0.0 17.9 jit_solution(12412423817610074251)
XLA Ops:
  0.0 16.9 %shard_map.46 = f32[288,8,128]{2,1,0:T(8,128)S(1)} custom-call(s32[4,24]{1,0:T(4,128)} %bitcast.6, s32[24]{0:T(128)} %bitcast.7, s32[2,8,128]{2,1,0:T(8,128)} %planes_in.1, f32[288,8,128]{2,1,0:T(8,128)} %bitcast.5), custom_call_target="tpu_custom_call" | custom-call | tf_op jit(solution)/shard_map/pallas_call | solution.py:408
  16.9 1.0 %copy.6 = f32[24,12,8,128]{3,2,1,0:T(8,128)} copy(f32[24,12,8,128]{3,2,1,0:T(8,128)S(1)} %bitcast.4) | data formatting | bytes 2359296

commit v7 on v6

--- a/solution.py
+++ b/solution.py
@@ -206,6 +206,9 @@
     def update(sums):
         coefs = tuple(SELF - TOTAL * s for s in sums)
         below, above = planes[0], planes[1]
+        part_lane, into_lane = (lax.broadcasted_iota(jnp.int32, (2 * cols, cols), d) for d in range(2))
+        apart = lax.rem(part_lane, cols) - into_lane
+        band = jnp.where((apart == 1) | (apart == -1), 1.0, 0.0).astype(jnp.bfloat16)
 
         def body(slot, carry):
             grain = grain_of(slot)
@@ -213,13 +216,16 @@
             small = [LINK * v for v in values]
             low = jnp.where(below == grain, LINK, 0.0)
             high = jnp.where(above == grain, LINK, 0.0)
+            stack = jnp.concatenate(small, axis=0)
+            big = stack.astype(jnp.bfloat16)
+            rest = (stack - big.astype(jnp.float32)).astype(jnp.bfloat16)
+            side = jnp.dot(jnp.concatenate([big, rest], axis=1), band, preferred_element_type=jnp.float32)
             for layer in range(depth):
                 v, w = values[layer], small[layer]
                 near = (
                     jnp.where(row == rows - 1, 0.0, pltpu.roll(w, rows - 1, 0))
                     + jnp.where(row == 0, 0.0, pltpu.roll(w, 1, 0))
-                    + jnp.where(col == cols - 1, 0.0, pltpu.roll(w, cols - 1, 1))
-                    + jnp.where(col == 0, 0.0, pltpu.roll(w, 1, 1))
+                    + side[rows * layer : rows * layer + rows]
                     + (small[layer - 1] if layer else low)
                     + (small[layer + 1] if layer < depth - 1 else high)
                 )

time: 18 us -> 18 us (level)
  no operation moved by 1% of the time
where the time goes in v7:
time: 18 us; the launch traced here: 17.9 us
  Pallas kernels  16.9 us (94%)
  local copies, waits for them, and re-layouts  1.02 us (6%)
    pallas_call x1, Pallas kernels, on_device(): pl.pallas_call(functools.partial(kernel, slots, depth, nx, ny), out_shape...  16.9 us
    unnamed x1, local copies, waits for them, and re-layouts  1.02 us

profile of v7, /device:TPU:1, one launch (start us, length us, event | category | flops | bytes accessed | tf_op | source)
XLA Modules:
  0.0 17.9 jit_solution(15874988253827163119)
XLA Ops:
  0.0 16.9 %shard_map.46 = f32[288,8,128]{2,1,0:T(8,128)S(1)} custom-call(s32[4,24]{1,0:T(4,128)} %bitcast.6, s32[24]{0:T(128)} %bitcast.7, s32[2,8,128]{2,1,0:T(8,128)} %planes_in.1, f32[288,8,128]{2,1,0:T(8,128)} %bitcast.5), custom_call_target="tpu_custom_call" | custom-call | tf_op jit(solution)/shard_map/pallas_call | solution.py:414
  16.9 1.0 %copy.6 = f32[24,12,8,128]{3,2,1,0:T(8,128)} copy(f32[24,12,8,128]{3,2,1,0:T(8,128)S(1)} %bitcast.4) | data formatting | bytes 2359296

commit v8 on v7

--- a/solution.py
+++ b/solution.py
@@ -245,14 +245,14 @@
                 rim_x[face, layer, k : k + 1] = field[tile(slot, layer), edge : edge + 1]
     for face in range(2, 4):
         rim_y[face - 2] = gather_columns(face, 0 if face == 2 else cols - 1, field)
-    pl.semaphore_wait(barrier, FACES)
-    for face in range(FACES):
-        copy(RIM, face).start()
     for face in range(2, 4):
         for other in range(2):
             rims = [rim_x[other, layer] for layer in range(depth)]
             cor_y[face - 2, other] = corners(rims, 0 if face == 2 else cols - 1)
-        copy(CORNER, face).start()
+    pl.semaphore_wait(barrier, FACES)
+    for kind, faces in ((RIM, (2, 3)), (CORNER, (2, 3)), (RIM, (0, 1))):
+        for face in faces:
+            copy(kind, face).start()
 
     loads[2].wait()
     loads[3].wait()
@@ -392,7 +392,7 @@
             out[at] = local[at] + halo[tile(held_pair, layer)]
         return carry
 
-    lax.fori_loop(0, slots, finish, 0)
+    lax.fori_loop(0, slots, finish, 0, unroll=UNROLL)
     for kind in (RIM, LOCAL, BEHIND, SUMS, CORNER):
         for face in range(FACES):
             copy(kind, face).wait_send()

time: 18 us -> 18 us (level)
  no operation moved by 1% of the time
where the time goes in v8:
time: 18 us; the launch traced here: 17.9 us
  Pallas kernels  16.8 us (93%)
  local copies, waits for them, and re-layouts  1.02 us (6%)
    pallas_call x1, Pallas kernels, on_device(): pl.pallas_call(functools.partial(kernel, slots, depth, nx, ny), out_shape...  16.8 us
    unnamed x1, local copies, waits for them, and re-layouts  1.02 us

profile of v8, /device:TPU:1, one launch (start us, length us, event | category | flops | bytes accessed | tf_op | source)
XLA Modules:
  0.0 17.9 jit_solution(1714838768029220211)
XLA Ops:
  0.0 16.8 %shard_map.46 = f32[288,8,128]{2,1,0:T(8,128)S(1)} custom-call(s32[4,24]{1,0:T(4,128)} %bitcast.6, s32[24]{0:T(128)} %bitcast.7, s32[2,8,128]{2,1,0:T(8,128)} %planes_in.1, f32[288,8,128]{2,1,0:T(8,128)} %bitcast.5), custom_call_target="tpu_custom_call" | custom-call | tf_op jit(solution)/shard_map/pallas_call | solution.py:414
  16.9 1.0 %copy.6 = f32[24,12,8,128]{3,2,1,0:T(8,128)} copy(f32[24,12,8,128]{3,2,1,0:T(8,128)S(1)} %bitcast.4) | data formatting | bytes 2359296
